TPU v7x, 256 devices: a whole 4x4x8 slice. The times are simulated.
256 devices in a mesh: ops: 4 (over x_lo, core), sec: 64 (over y, x_hi, z).
Axes of the slice: x: 4 (x_hi: 2, x_lo: 2; x = x_hi * 2 + x_lo), y: 4, z: 8, core: 2. Of those that a mesh axis runs over, the one named last changes fastest.
Arguments:
- wavefunction: bfloat16 [2, 256, 256, 256], P(None, 'sec')
- left_blocks: bfloat16 [40, 256, 256, 256], P('ops', 'sec'), may hold values from -0.0625 to 0.0625
- right_blocks: bfloat16 [40, 256, 256, 256], P('ops', 'sec'), may hold values from -0.375 to 0.375
- pairing: int32 [40, 256], P('ops', 'sec'), may hold values from 0 to 255, as said below
- sector_dims: int32 [2, 256], replicated, may hold values from 1 to 256, as said below
Outputs:
- sigma: float32 [2, 256, 256, 256], P(None, 'sec', 'ops')
Inputs may be any that keep to these rules, and one draw needn't show every extreme that they name: pairing[t, l] differs from l by at most 4, and by exactly 4 for some term. `sector_dims`: each side has some sector of dimension 256.
All inputs are finite; a program needn't handle non-finite values.
Results may differ from a plain program's by a relative error of at most 0.0029.
Values sent between devices are 32-bit elements; how exact they have to be, the bound alone decides.
No kernel may reach another device: no remote copies, remote signals or barrier semaphores. Data moves between devices by JAX's collectives and lax.ppermute only.
A program may use at most 192 MiB of HBM per device.

v0:
```python
import jax
import jax.numpy as jnp
from jax import lax
from jax.sharding import PartitionSpec as P


def shifted(shard, axis, by):
    peers = lax.axis_size(axis)
    pairs = [(i, i + by) for i in range(peers) if 0 <= i + by < peers]
    return lax.ppermute(shard, axis, pairs)


def body(wavefunction, left_blocks, right_blocks, pairing, sector_dims):
    sector_per_device = wavefunction.shape[1]
    pad_size = wavefunction.shape[2]
    first_sector = lax.axis_index("sec") * sector_per_device
    row_ids = jnp.arange(pad_size, dtype=jnp.int32)
    local_dims = lax.dynamic_slice_in_dim(sector_dims, first_sector, sector_per_device, 1)
    valid_mask = (row_ids[None, :, None] < local_dims[0][:, None, None]) & (
        row_ids[None, None, :] < local_dims[1][:, None, None]
    )
    masked = jnp.where(valid_mask[None], wavefunction, jnp.zeros((), wavefunction.dtype))
    partial_product = jnp.einsum(
        "vlab,tlcb->vtlac", masked, right_blocks, preferred_element_type=jnp.float32
    ).astype(jnp.bfloat16)
    term_contribution = jnp.einsum(
        "tlac,vtlcb->vtlab", left_blocks, partial_product, preferred_element_type=jnp.float32
    )
    position_index = pairing - first_sector + sector_per_device
    onehot = (
        position_index[:, :, None]
        == jnp.arange(3 * sector_per_device, dtype=jnp.int32)[None, None, :]
    ).astype(jnp.float32)
    spread = jnp.einsum("tls,vtlab->vsab", onehot, term_contribution, precision=lax.Precision.HIGH)
    from_below = shifted(spread[:, 2 * sector_per_device :], "sec", 1)
    from_above = shifted(spread[:, :sector_per_device], "sec", -1)
    local_blocks = spread[:, sector_per_device : 2 * sector_per_device] + from_below + from_above
    block_rows = lax.psum_scatter(local_blocks, "ops", scatter_dimension=2, tiled=True)
    row_share = pad_size // lax.axis_size("ops")
    share_ids = lax.axis_index("ops") * row_share + jnp.arange(row_share, dtype=jnp.int32)
    output_mask = (share_ids[None, :, None] < local_dims[0][:, None, None]) & (
        row_ids[None, None, :] < local_dims[1][:, None, None]
    )
    return jnp.where(output_mask[None], block_rows, jnp.zeros((), jnp.float32))


def solution(mesh):
    placed = (
        P(None, "sec", None, None),
        P("ops", "sec", None, None),
        P("ops", "sec", None, None),
        P("ops", "sec"),
        P(),
    )
    return jax.shard_map(
        body, mesh=mesh, in_specs=placed, out_specs=P(None, "sec", "ops", None), check_vma=False
    )
```

profile of v0, /device:TPU:1, one launch (start us, length us, event | category | flops | bytes accessed | tf_op | source)
XLA Modules:
  0.0 187.7 jit_solution(16610914746007531172)
XLA Ops:
  6.5 0.0 copy-start
  6.5 0.0 reduce-scatter.5.cloned.1.call-start
  6.5 0.7 copy-done
  7.2 0.1 constant_dynamic-slice_fusion
  7.3 0.1 iota_compare_fusion.1
  7.4 0.2 broadcast_and_fusion
  7.6 9.7 %convert_bitcast_fusion = bf16[2,10,4,256,256]{4,3,1,0,2:T(8,128)(2,1)} fusion(bf16[10,4,256,256]{3,2,1,0:T(8,128)(2,1)} %param.7, bf16[2,4,256,256]{3,2,1,0:T(8,128)(2,1)} %param.5, pred[4,256,256]{2,1,0:T(8,128)(4,1)S(1)} %broadcast_and_fusion), kind=kOutput, calls=%fused_computation.2 | convolution fusion | flops 2690121728 | bytes 17039360 | tf_op jit(solution)/shard_map/vlab,tlcb->vtlac/dot_general | solution.py:23
  17.3 12.7 %fusion.2 = f32[2,10,4,256,256]{3,4,0,2,1:T(8,128)} fusion(bf16[2,10,4,256,256]{4,3,1,0,2:T(8,128)(2,1)} %convert_bitcast_fusion, bf16[10,4,256,256]{3,2,1,0:T(8,128)(2,1)} %param.6), kind=kOutput, calls=%fused_computation.3 | convolution fusion | flops 2684354560 | bytes 36700160 | tf_op jit(solution)/shard_map/tlac,vtlcb->vtlab/dot_general | solution.py:26
  30.0 0.0 copy-start.2
  30.0 32.7 %copy.11 = f32[2,10,4,256,256]{4,1,2,3,0:T(8,128)} copy(f32[2,10,4,256,256]{3,4,0,2,1:T(8,128)} %fusion.2) | data formatting | bytes 41943040 | tf_op jit(solution)/shard_map/tlac,vtlcb->vtlab/transpose | solution.py:26
  62.7 0.0 copy-done.2
  62.7 16.9 %convolution_bitcast_fusion = f32[2,12,256,256]{3,1,2,0:T(8,128)} fusion(f32[2,10,4,256,256]{4,1,2,3,0:T(8,128)} %copy.11, s32[10,4]{0,1:T(4,128)S(1)} %subtract_add_fusion), kind=kOutput, calls=%fused_computation.6 | convolution fusion | flops 377487840 | bytes 27263136 | tf_op jit(solution)/shard_map/tls,vtlab->vsab/dot_general | solution.py:34
  79.6 4.0 %fusion.12 = (f32[2,4,256,256]{3,1,2,0:T(4,128)S(1)}, f32[2,4,256,256]{3,1,2,0:T(4,128)S(1)}) fusion(f32[2,12,256,256]{3,1,2,0:T(8,128)} %convolution_bitcast_fusion), kind=kLoop, calls=%fused_computation.26 | loop fusion | bytes 8388608 | tf_op jit(solution)/shard_map/slice | solution.py:35
  83.6 4.5 %collective-permute-start = (f32[2,4,256,256]{3,1,2,0:T(4,128)S(1)}, f32[2,4,256,256]{3,1,2,0:T(4,128)S(1)}, u32[]{:S(2)}, u32[]{:S(2)}) collective-permute-start(f32[2,4,256,256]{3,1,2,0:T(4,128)S(1)} %get-tuple-element.5), channel_id=1, source_target_pairs={{0,1},{1,2},{2,3},{3,4},{4,5},{5,6},{6,7},{7,8},{8,9},{9,10},{10,1... | collective-permute-start | bytes 6291464 | tf_op jit(solution)/shard_map/ppermute | solution.py:10
  88.2 1.3 collective-permute-start.1
  89.5 42.8 %collective-permute-done = f32[2,4,256,256]{3,1,2,0:T(4,128)S(1)} collective-permute-done((f32[2,4,256,256]{3,1,2,0:T(4,128)S(1)}, f32[2,4,256,256]{3,1,2,0:T(4,128)S(1)}, u32[]{:S(2)}, u32[]{:S(2)}) %collective-permute-start) | collective-permute-done | bytes 2097184 | tf_op jit(solution)/shard_map/ppermute | solution.py:10
  132.3 4.1 %collective-permute-done.1 = f32[2,4,256,256]{3,1,2,0:T(4,128)S(1)} collective-permute-done((f32[2,4,256,256]{3,1,2,0:T(4,128)S(1)}, f32[2,4,256,256]{3,1,2,0:T(4,128)S(1)}, u32[]{:S(2)}, u32[]{:S(2)}) %collective-permute-start.1) | collective-permute-done | bytes 2097184 | tf_op jit(solution)/shard_map/ppermute | solution.py:10
  136.4 0.0 copy-start.1
  136.4 3.2 %copy_bitcast_fusion = f32[256,2,4,256]{3,2,1,0:T(4,128)S(1)} fusion(f32[2,4,256,256]{3,1,2,0:T(4,128)S(1)} %collective-permute-done.1, f32[2,4,256,256]{3,1,2,0:T(4,128)S(1)} %collective-permute-done, f32[2,12,256,256]{3,1,2,0:T(8,128)} %convolution_bitcast_fusion), kind=kLoop, calls=%fused_computation.9 | loop fusion | flops 1048576 | bytes 8388608
  139.6 2.1 %reshape.99 = f32[256,2048]{1,0:T(8,128)} reshape(f32[256,2,4,256]{3,2,1,0:T(4,128)S(1)} %copy_bitcast_fusion) | data formatting | bytes 4194304
  141.7 0.0 reduce-scatter.5.cloned.1.call-update
  141.8 0.1 broadcast_compare_fusion
  141.8 0.1 broadcast_and_fusion.1
  142.0 36.4 %reduce-scatter.5.cloned.1.call-done = f32[64,2048]{1,0:T(8,128)} async-done(((f32[256,2048]{1,0:T(8,128)}), f32[64,2048]{1,0:T(8,128)}) %reduce-scatter.5.cloned.1.call-update) | async-done | bytes 524304
  178.4 1.4 reshape.100
  179.8 0.2 copy_select_fusion
  180.0 0.9 copy.12
  180.8 0.0 copy-done.1
  (3 shorter events, 0.0 us)
Async XLA Ops:
  6.5 0.7 copy-start
  6.5 171.8 %reduce-scatter.5.cloned.1.call-start = ((), (), s32[]{:S(2)}) async-start(), calls=%async_computation.1 | async-start | bytes 2621440
  30.0 32.8 %copy-start.2 = (s32[10,4]{0,1:T(4,128)S(1)}, s32[10,4]{0,1:T(4,128)}, u32[]{:S(2)}) copy-start(s32[10,4]{0,1:T(4,128)} %param.8) | copy-start | bytes 484
  83.6 48.7 %collective-permute-start = (f32[2,4,256,256]{3,1,2,0:T(4,128)S(1)}, f32[2,4,256,256]{3,1,2,0:T(4,128)S(1)}, u32[]{:S(2)}, u32[]{:S(2)}) collective-permute-start(f32[2,4,256,256]{3,1,2,0:T(4,128)S(1)} %get-tuple-element.5), channel_id=1, source_target_pairs={{0,1},{1,2},{2,3},{3,4},{4,5},{5,6},{6,7},{7,8},{8,9},{9,10},{10,1... | collective-permute-start | bytes 6291464 | tf_op jit(solution)/shard_map/ppermute | solution.py:10
  88.2 48.2 %collective-permute-start.1 = (f32[2,4,256,256]{3,1,2,0:T(4,128)S(1)}, f32[2,4,256,256]{3,1,2,0:T(4,128)S(1)}, u32[]{:S(2)}, u32[]{:S(2)}) collective-permute-start(f32[2,4,256,256]{3,1,2,0:T(4,128)S(1)} %get-tuple-element.6), channel_id=1, source_target_pairs={{1,0},{2,1},{3,2},{4,3},{5,4},{6,5},{7,6},{8,7},{9,8},{10,9},{11,1... | collective-permute-start | bytes 6291464 | tf_op jit(solution)/shard_map/ppermute | solution.py:10
  136.4 44.5 %copy-start.1 = (s32[2,256]{1,0:T(2,128)S(1)}, s32[2,256]{1,0:T(2,128)}, u32[]{:S(2)}) copy-start(s32[2,256]{1,0:T(2,128)} %param.9) | copy-start | bytes 6148
Sparse Core Ops, SparseCore 0:
  141.9 36.4 reduce-scatter.4
where the time goes:
time: 189 us; the launch traced here: 188 us
  waiting for transfers between devices  83.3 us (44%)
  local copies, waits for them, and re-layouts  41.9 us (22%)
  matrix products  39.3 us (21%)
  between operations  13.5 us (7%)
  starting transfers between devices  5.8 us (3%)
  other arithmetic  3.89 us (2%)
    ppermute x2, waiting for transfers between devices, shifted(): return lax.ppermute(shard, axis, pairs)  46.9 us
    unnamed x2, waiting for transfers between devices  36.4 us
    transpose x1, local copies, waits for them, and re-layouts, body(): jnp.einsum('tlac,vtlcb->vtlab', left_blocks, partial_product, preferred_e...  32.7 us
    dot_general x1, matrix products, body(): jnp.einsum('tls,vtlab->vsab', onehot, term_contribution, precision=lax.Pr...  16.9 us
    dot_general x1, matrix products, body(): jnp.einsum('tlac,vtlcb->vtlab', left_blocks, partial_product, preferred_e...  12.7 us
    dot_general x1, matrix products, body(): jnp.einsum('vlab,tlcb->vtlac', masked, right_blocks, preferred_element_ty...  9.73 us
    ppermute x2, starting transfers between devices, shifted(): return lax.ppermute(shard, axis, pairs)  5.79 us
    unnamed x8, local copies, waits for them, and re-layouts  4.21 us
  transfers between devices with their start and end apart: 3, of which 3 were waited for; matrix products, arithmetic and copies ran while one was open for 0% of the time, Pallas kernels for 0%

commit v1 on v0

v1 whole, which is shorter than its diff:
```python
import functools

import jax
import jax.numpy as jnp
from jax import lax
from jax.experimental import pallas as pl
from jax.experimental.pallas import tpu as pltpu
from jax.sharding import PartitionSpec as P

Z_RUN = 8
BOTH = ("ops", "sec")
UNROLL = 5


def terms_kernel(
    vectors, halo, me_ref, dims_hbm, pair_hbm, wave_ref, left_ref, right_ref, *refs
):
    number = len(vectors)
    keep_refs, send_refs = refs[: 2 * number : 2], refs[1 : 2 * number : 2]
    (
        wave_buf, masked, left_buf, right_buf, half, dims_ref, pair_ref, code_ref,
        wave_sem, left_sem, right_sem, dims_sem, pair_sem,
    ) = refs[2 * number :]
    terms, sectors, pad, _ = left_ref.shape
    pairs = terms * sectors
    run = pad // 4
    peers = dims_ref.shape[1] // sectors
    me = me_ref[0]
    sec, ops = me % peers, me // peers
    core, x_lo = ops % 2, ops // 2
    first = sec * sectors
    z = sec % Z_RUN

    dims_copy = pltpu.make_async_copy(dims_hbm, dims_ref, dims_sem)
    pair_copy = pltpu.make_async_copy(pair_hbm, pair_ref, pair_sem)
    pair_copy.start()
    dims_copy.start()
    wave_copies = [
        pltpu.make_async_copy(wave_ref.at[v], wave_buf.at[j], wave_sem.at[j])
        for j, v in enumerate(vectors)
    ]
    for copy in wave_copies:
        copy.start()
    for keep_ref, send_ref in zip(keep_refs, send_refs):
        keep_ref[...] = jnp.zeros_like(keep_ref)
        send_ref[...] = jnp.zeros_like(send_ref)
    left_buf[pairs] = jnp.zeros((pad, pad), jnp.bfloat16)
    right_buf[pairs] = jnp.zeros((pad, pad), jnp.bfloat16)
    pair_copy.wait()

    def left_copy(t, l, i):
        return pltpu.make_async_copy(left_ref.at[t, l], left_buf.at[i], left_sem.at[i])

    def right_copy(t, l, i):
        return pltpu.make_async_copy(right_ref.at[t, l], right_buf.at[i], right_sem.at[i])

    def scan(t, count):
        for l in range(sectors):
            place = pair_ref[l, t] - first
            outside = (place < 0) | (place >= sectors)
            take = outside if halo else jnp.logical_not(outside)

            @pl.when(take)
            def _():
                code_ref[count] = count * 1024 + l * 64 + place + sectors
                right_copy(t, l, count).start()
                left_copy(t, l, count).start()

            count = count + take.astype(jnp.int32)
        return count

    count = lax.fori_loop(0, terms, scan, jnp.int32(0))
    for u in range(UNROLL - 1):
        code_ref[count + u] = pairs * 1024 + sectors

    dims_copy.wait()
    for copy in wave_copies:
        copy.wait()
    rows = lax.broadcasted_iota(jnp.int32, (pad, pad), 0)
    cols = lax.broadcasted_iota(jnp.int32, (pad, pad), 1)
    for l in range(sectors):
        valid = (rows < dims_ref[0, first + l]) & (cols < dims_ref[1, first + l])
        for j in range(number):
            value = jnp.where(valid, wave_buf[j, l].astype(jnp.float32), 0.0)
            masked[l, j * pad : (j + 1) * pad] = value.astype(jnp.bfloat16)

    def first_stage(u, i):
        code = code_ref[i]
        product = lax.dot_general(
            masked[code % 1024 // 64], right_buf[code // 1024], (((1,), (1,)), ((), ())),
            preferred_element_type=jnp.float32,
        )
        half[u] = product.astype(jnp.bfloat16)

    def second_stage(u, i):
        code = code_ref[i]
        place = code % 64 - sectors
        if halo:
            at = jnp.where(place < 0, place + sectors, place)
            flip = jnp.where(place < 0, z == 0, z == Z_RUN - 1).astype(jnp.int32)
        else:
            at, flip = place, 0
        near = x_lo ^ flip
        blocks = [2 * near + core, 2 * (1 - near) + core, 2 * near + 1 - core, 2 * (1 - near) + 1 - core]
        lhs = jnp.concatenate(
            [left_buf[code // 1024, pl.ds(pl.multiple_of(b * run, run), run), :] for b in blocks], axis=0
        )
        for j in range(number):
            term = lax.dot_general(
                lhs, half[u, j * pad : (j + 1) * pad], (((1,), (0,)), ((), ())),
                preferred_element_type=jnp.float32,
            )
            for q in range(2):
                keep_refs[j][q, at] += term[q * run : (q + 1) * run]
                send_refs[j][q, at] += term[(2 + q) * run : (3 + q) * run]

    def step(k, carry):
        base = k * UNROLL
        for u in range(UNROLL):

            @pl.when(base + u < count)
            def _():
                right_copy(0, 0, base + u).wait()
                left_copy(0, 0, base + u).wait()

        first_stage(0, base)
        for u in range(UNROLL):
            if u + 1 < UNROLL:
                first_stage(u + 1, base + u + 1)
            second_stage(u, base + u)
        return carry

    lax.fori_loop(0, (count + UNROLL - 1) // UNROLL, step, 0)


def terms_call(vectors, halo, me, dims, pairing, wave, left, right):
    terms, sectors, pad, _ = left.shape
    number = len(vectors)
    pairs = terms * sectors
    places = 2 * sectors if halo else sectors
    shape = jax.ShapeDtypeStruct((2, places, pad // 4, pad), jnp.float32)
    in_hbm = pl.BlockSpec(memory_space=pltpu.HBM)
    vmem = pl.BlockSpec(memory_space=pltpu.VMEM)
    operands = (dims, pairing.T, wave, left, right)
    return pl.pallas_call(
        functools.partial(terms_kernel, vectors, halo),
        out_shape=(shape,) * (2 * number),
        in_specs=[pl.BlockSpec(memory_space=pltpu.SMEM)] + [in_hbm] * 5,
        out_specs=(vmem,) * (2 * number),
        scratch_shapes=[
            pltpu.VMEM((number, sectors, pad, pad), jnp.bfloat16),
            pltpu.VMEM((sectors, number * pad, pad), jnp.bfloat16),
            pltpu.VMEM((pairs + 1, pad, pad), jnp.bfloat16),
            pltpu.VMEM((pairs + 1, pad, pad), jnp.bfloat16),
            pltpu.VMEM((UNROLL, number * pad, pad), jnp.bfloat16),
            pltpu.SMEM(dims.shape, jnp.int32),
            pltpu.SMEM((sectors, terms), jnp.int32),
            pltpu.SMEM((pairs + UNROLL - 1,), jnp.int32),
            pltpu.SemaphoreType.DMA((number,)),
            pltpu.SemaphoreType.DMA((pairs,)),
            pltpu.SemaphoreType.DMA((pairs,)),
            pltpu.SemaphoreType.DMA,
            pltpu.SemaphoreType.DMA,
        ],
        compiler_params=pltpu.CompilerParams(vmem_limit_bytes=32 * 1024 * 1024),
        cost_estimate=pl.CostEstimate(
            flops=pairs // 2 * number * 4 * pad**3, bytes_accessed=pairs * pad * pad * 2, transcendentals=0
        ),
        name="halo_terms" if halo else "own_terms",
    )(me.reshape(1), *(pltpu.with_memory_space_constraint(x, pltpu.HBM) for x in operands))


def body(wavefunction, left_blocks, right_blocks, pairing, sector_dims):
    sectors, pad = wavefunction.shape[1:3]
    ops, sec = lax.axis_index("ops"), lax.axis_index("sec")
    peers = lax.axis_size("sec")
    other_core = [(i, i ^ 1) for i in range(4)]
    other_chip = [(i, i ^ 2) for i in range(4)]
    upward = [
        (o * peers + s, (o ^ 2 if s % Z_RUN == Z_RUN - 1 else o) * peers + (s + 1) % peers)
        for o in range(4)
        for s in range(peers)
    ]
    downward = [(b, a) for a, b in upward]

    def terms(vectors, halo, pairing):
        return terms_call(
            vectors, halo, lax.axis_index(BOTH), sector_dims, pairing, wavefunction, left_blocks, right_blocks
        )

    def to_core(x):
        return lax.ppermute(x, "ops", other_core)

    def to_chip(x):
        return lax.ppermute(x, "ops", other_chip)

    keep0, send0, keep1, send1 = terms((0, 1), True, pairing)
    recv0 = to_core(send0)
    recv1 = to_core(send1)
    halo0 = keep0 + recv0
    far1 = keep1[1] + recv1[1]
    halo0, far1, pairing_later = lax.optimization_barrier((halo0, far1, pairing))
    down0, up0 = halo0[:, :sectors], halo0[:, sectors:]
    below0 = lax.ppermute(up0, BOTH, upward)
    above0 = lax.ppermute(down0, BOTH, downward)
    far1 = to_chip(far1)
    halo1 = keep1[0] + recv1[0] + far1
    below1 = lax.ppermute(halo1[sectors:], BOTH, upward)
    above1 = lax.ppermute(halo1[:sectors], BOTH, downward)

    own0, give0, own1, give1 = terms((0, 1), False, pairing_later)
    got1 = to_core(give1)
    got0 = to_core(give0)
    own_far1 = to_chip(own1[1] + got1[1])
    far0 = to_chip(own0[1] + got0[1] + below0[1] + above0[1])
    out0 = own0[0] + got0[0] + below0[0] + above0[0] + far0
    out1 = own1[0] + got1[0] + own_far1 + below1 + above1

    local_dims = lax.dynamic_slice_in_dim(sector_dims, sec * sectors, sectors, 1)
    share_ids = ops * (pad // 4) + jnp.arange(pad // 4, dtype=jnp.int32)
    col_ids = jnp.arange(pad, dtype=jnp.int32)
    valid = (share_ids[None, :, None] < local_dims[0][:, None, None]) & (
        col_ids[None, None, :] < local_dims[1][:, None, None]
    )
    return jnp.where(valid[None], jnp.stack([out0, out1]), jnp.zeros((), jnp.float32))


def solution(mesh):
    placed = (
        P(None, "sec", None, None),
        P("ops", "sec", None, None),
        P("ops", "sec", None, None),
        P("ops", "sec"),
        P(),
    )
    return jax.shard_map(
        body, mesh=mesh, in_specs=placed, out_specs=P(None, "sec", "ops", None), check_vma=False
    )
```

time: 189 us -> 70 us (0.37)
  waiting for transfers between devices: 83.3 us -> 30.7 us
  local copies, waits for them, and re-layouts: 41.9 us -> 0.19 us
  matrix products: 39.3 us -> 0 us
  Pallas kernels: 0 us -> 16.4 us
  between operations: 13.5 us -> 0.1 us
  starting transfers between devices: 5.8 us -> 17.2 us
    dot_general x3 -> x0, matrix products: 39.3 us -> none  [the longest x1 16.9 us: body(): jnp.einsum('tls,vtlab->vsab', onehot, term_contribution, precision=lax.Pr...]
    unnamed x2 -> x0, waiting for transfers between devices: 36.4 us -> none
    transpose x1 -> x0, local copies, waits for them, and re-layouts: 32.7 us -> none  [body(): jnp.einsum('tlac,vtlcb->vtlab', left_blocks, partial_product, preferred_e...]
    pallas_call x0 -> x2, Pallas kernels: none -> 16.4 us  [terms_call(): pl.pallas_call(functools.partial(terms_kernel, vectors, halo), out_shape=...]
    ppermute x2 -> x11, waiting for transfers between devices: 46.9 us -> 30.7 us  [the longest x1 8.81 us: body(): above0 = lax.ppermute(down0, BOTH, downward)]
    ppermute x2 -> x11, starting transfers between devices: 5.79 us -> 17.2 us  [the longest x1 8.6 us: body(): above0 = lax.ppermute(down0, BOTH, downward)]
    unnamed x8 -> x2, local copies, waits for them, and re-layouts: 4.21 us -> 0.01 us
    slice x1 -> x2, local copies, waits for them, and re-layouts: 4.01 us -> 0.11 us  [the longest x1 0.07 us: body(): down0, up0 = (halo0[:, :sectors], halo0[:, sectors:])]
  transfers between devices with their start and end apart: 3 -> 11, of which waited for: 3 -> 6; matrix products, arithmetic and copies ran while one was open for 0% -> 4% of each run, Pallas kernels for 0% -> 0%
where the time goes in v1:
time: 70 us; the launch traced here: 69.6 us
  waiting for transfers between devices  30.7 us (44%)
  starting transfers between devices  17.2 us (25%)
  Pallas kernels  16.4 us (23%)
  other arithmetic  5.01 us (7%)
    pallas_call x2, Pallas kernels, terms_call(): pl.pallas_call(functools.partial(terms_kernel, vectors, halo), out_shape=...  16.4 us
    ppermute x1, waiting for transfers between devices, body(): above0 = lax.ppermute(down0, BOTH, downward)  8.81 us
    ppermute x1, starting transfers between devices, body(): above0 = lax.ppermute(down0, BOTH, downward)  8.6 us
    ppermute x1, waiting for transfers between devices, body(): below0 = lax.ppermute(up0, BOTH, upward)  7.31 us
    ppermute x1, waiting for transfers between devices, body(): below1 = lax.ppermute(halo1[sectors:], BOTH, upward)  6.77 us
    ppermute x4, starting transfers between devices, to_core(): return lax.ppermute(x, 'ops', other_core)  4.85 us
    ppermute x1, waiting for transfers between devices, body(): above1 = lax.ppermute(halo1[:sectors], BOTH, downward)  3 us
    ppermute x4, waiting for transfers between devices, to_core(): return lax.ppermute(x, 'ops', other_core)  2.86 us
  transfers between devices with their start and end apart: 11, of which 6 were waited for; matrix products, arithmetic and copies ran while one was open for 4% of the time, Pallas kernels for 0%

profile of v1, /device:TPU:1, one launch (start us, length us, event | category | flops | bytes accessed | tf_op | source)
XLA Modules:
  0.0 69.6 jit_solution(6150393653095300733)
XLA Ops:
  0.0 0.0 copy-start
  0.0 7.1 %halo_terms.1 = (f32[2,8,64,256]{3,2,1,0:T(8,128)S(1)}, f32[2,8,64,256]{3,2,1,0:T(8,128)}, f32[2,8,64,256]{3,2,1,0:T(8,128)S(1)}, f32[2,8,64,256]{3,2,1,0:T(8,128)S(1)}) custom-call(s32[1]{0:T(128)} %bitcast.2.me_ref, s32[2,256]{1,0:T(2,128)} %dims_hbm.3, s32[4,10]{1,0:T(4,128)} %bitcast.37, bf16[2,4,256,256]{3,2,1,0:T(8,128)(2,1)} %wave_ref.3, ...), custom_call_target="tpu_custom_call" | custom-call | flops 2684354560 | bytes 5242880 | tf_op jit(solution)/shard_map/halo_terms/pallas_call | solution.py:145
  7.1 3.3 %collective-permute-start = (f32[2,8,64,256]{3,2,1,0:T(8,128)}, f32[2,8,64,256]{3,2,1,0:T(8,128)}, u32[]{:S(2)}, u32[]{:S(2)}) collective-permute-start(f32[2,8,64,256]{3,2,1,0:T(8,128)} %get-tuple-element.17), channel_id=1, source_target_pairs={{0,64},{64,0},{128,192},{192,128},{1,65},{65,1},{129,193},{193,129... | collective-permute-start | bytes 3145736 | tf_op jit(solution)/shard_map/ppermute | solution.py:192
  10.4 0.1 collective-permute-start.1
  10.5 0.0 copy-done
  10.5 0.1 constant_dynamic-slice_fusion
  10.6 0.1 iota_compare_fusion
  10.7 2.9 %collective-permute-done = f32[2,8,64,256]{3,2,1,0:T(8,128)} collective-permute-done((f32[2,8,64,256]{3,2,1,0:T(8,128)}, f32[2,8,64,256]{3,2,1,0:T(8,128)}, u32[]{:S(2)}, u32[]{:S(2)}) %collective-permute-start) | collective-permute-done | bytes 1048608 | tf_op jit(solution)/shard_map/ppermute | solution.py:192
  13.5 1.4 %add.91 = f32[2,8,64,256]{3,2,1,0:T(8,128)S(1)} add(f32[2,8,64,256]{3,2,1,0:T(8,128)S(1)} %get-tuple-element.16, f32[2,8,64,256]{3,2,1,0:T(8,128)} %collective-permute-done) | non-fusion elementwise | flops 262144 | bytes 3145728 | tf_op jit(solution)/shard_map/add | solution.py:200
  14.9 0.0 collective-permute-done.1
  14.9 1.1 %fusion.2 = f32[8,64,256]{2,1,0:T(8,128)S(1)} fusion(f32[2,8,64,256]{3,2,1,0:T(8,128)} %collective-permute-done.1, f32[2,8,64,256]{3,2,1,0:T(8,128)S(1)} %get-tuple-element.18), kind=kLoop, calls=%fused_computation.4 | loop fusion | flops 131072 | bytes 1572864 | tf_op jit(solution)/shard_map/add | solution.py:201
  16.0 9.4 %own_terms.1 = (f32[2,4,64,256]{3,2,1,0:T(8,128)S(1)}, f32[2,4,64,256]{3,2,1,0:T(8,128)S(1)}, f32[2,4,64,256]{3,2,1,0:T(8,128)S(1)}, f32[2,4,64,256]{3,2,1,0:T(8,128)S(1)}) custom-call(s32[1]{0:T(128)} %bitcast.2.me_ref, s32[2,256]{1,0:T(2,128)} %dims_hbm.3, s32[4,10]{1,0:T(4,128)} %bitcast.38, bf16[2,4,256,256]{3,2,1,0:T(8,128)(2,1)} %wave_ref.3, ...), custom_call_target="tpu_custom_call" | custom-call | flops 2684354560 | bytes 5242880 | tf_op jit(solution)/shard_map/own_terms/pallas_call | solution.py:145
  25.4 0.1 fusion.13
  25.4 8.6 %collective-permute-start.4 = (f32[2,4,64,256]{3,2,1,0:T(8,128)S(1)}, f32[2,4,64,256]{3,2,1,0:T(8,128)S(1)}, u32[]{:S(2)}, u32[]{:S(2)}) collective-permute-start(f32[2,4,64,256]{3,2,1,0:T(8,128)S(1)} %get-tuple-element.28), channel_id=1, source_target_pairs={{1,0},{2,1},{3,2},{4,3},{5,4},{6,5},{7,6},{136,7},{9,8},{10,9},{11... | collective-permute-start | bytes 1572872 | tf_op jit(solution)/shard_map/ppermute | solution.py:205
  34.0 0.0 collective-permute-start.3
  34.0 0.6 collective-permute-start.2
  34.7 0.5 collective-permute-start.8
  35.2 0.1 broadcast_compare_fusion
  35.3 0.1 broadcast_and_fusion
  35.4 0.8 %collective-permute-start.6 = (f32[2,4,64,256]{3,2,1,0:T(8,128)S(1)}, f32[2,4,64,256]{3,2,1,0:T(8,128)S(1)}, u32[]{:S(2)}, u32[]{:S(2)}) collective-permute-start(f32[2,4,64,256]{3,2,1,0:T(8,128)S(1)} %get-tuple-element.25), channel_id=1, source_target_pairs={{0,64},{64,0},{128,192},{192,128},{1,65},{65,1},{129,193},{193,129... | collective-permute-start | bytes 1572872 | tf_op jit(solution)/shard_map/ppermute | solution.py:192
  36.2 8.8 %collective-permute-done.4 = f32[2,4,64,256]{3,2,1,0:T(8,128)S(1)} collective-permute-done((f32[2,4,64,256]{3,2,1,0:T(8,128)S(1)}, f32[2,4,64,256]{3,2,1,0:T(8,128)S(1)}, u32[]{:S(2)}, u32[]{:S(2)}) %collective-permute-start.4) | collective-permute-done | bytes 524320 | tf_op jit(solution)/shard_map/ppermute | solution.py:205
  45.0 7.3 %collective-permute-done.3 = f32[2,4,64,256]{3,2,1,0:T(8,128)S(1)} collective-permute-done((f32[2,4,64,256]{3,2,1,0:T(8,128)S(1)}, f32[2,4,64,256]{3,2,1,0:T(8,128)S(1)}, u32[]{:S(2)}, u32[]{:S(2)}) %collective-permute-start.3) | collective-permute-done | bytes 524320 | tf_op jit(solution)/shard_map/ppermute | solution.py:204
  52.3 0.0 collective-permute-done.2
  52.3 0.1 fusion.9
  52.4 1.0 %collective-permute-start.5 = (f32[4,64,256]{2,1,0:T(8,128)S(1)}, f32[4,64,256]{2,1,0:T(8,128)S(1)}, u32[]{:S(2)}, u32[]{:S(2)}) collective-permute-start(f32[4,64,256]{2,1,0:T(8,128)S(1)} %fusion.9), channel_id=1, source_target_pairs={{0,128},{64,192},{128,0},{192,64},{1,129},{65,193},{129,1},{193,65... | collective-permute-start | bytes 786440 | tf_op jit(solution)/shard_map/ppermute | solution.py:195
  53.4 0.0 collective-permute-done.8
  53.4 1.1 %fusion.1 = f32[8,64,256]{2,1,0:T(8,128)S(1)} fusion(f32[8,64,256]{2,1,0:T(8,128)S(1)} %collective-permute-done.8, f32[2,8,64,256]{3,2,1,0:T(8,128)} %collective-permute-done.1, f32[2,8,64,256]{3,2,1,0:T(8,128)S(1)} %get-tuple-element.18), kind=kLoop, calls=%fused_computation.2 | loop fusion | flops 262144 | bytes 2097152 | tf_op jit(solution)/shard_map/add | solution.py:207
  54.6 2.1 %collective-permute-start.10 = (f32[4,64,256]{2,1,0:T(8,128)S(1)}, f32[4,64,256]{2,1,0:T(8,128)S(1)}, u32[]{:S(2)}, u32[]{:S(2)}) collective-permute-start(f32[4,64,256]{2,1,0:T(8,128)S(1)} %get-tuple-element.30), channel_id=1, source_target_pairs={{1,0},{2,1},{3,2},{4,3},{5,4},{6,5},{7,6},{136,7},{9,8},{10,9},{11... | collective-permute-start | bytes 786440 | tf_op jit(solution)/shard_map/ppermute | solution.py:209
  56.7 0.0 collective-permute-start.9
  56.7 0.0 collective-permute-done.6
  56.7 0.1 collective-permute-start.7
  56.8 1.9 %collective-permute-done.5 = f32[4,64,256]{2,1,0:T(8,128)S(1)} collective-permute-done((f32[4,64,256]{2,1,0:T(8,128)S(1)}, f32[4,64,256]{2,1,0:T(8,128)S(1)}, u32[]{:S(2)}, u32[]{:S(2)}) %collective-permute-start.5) | collective-permute-done | bytes 262176 | tf_op jit(solution)/shard_map/ppermute | solution.py:195
  58.7 0.1 fusion.12
  58.8 3.0 %collective-permute-done.10 = f32[4,64,256]{2,1,0:T(8,128)S(1)} collective-permute-done((f32[4,64,256]{2,1,0:T(8,128)S(1)}, f32[4,64,256]{2,1,0:T(8,128)S(1)}, u32[]{:S(2)}, u32[]{:S(2)}) %collective-permute-start.10) | collective-permute-done | bytes 262176 | tf_op jit(solution)/shard_map/ppermute | solution.py:209
  61.8 6.8 %collective-permute-done.9 = f32[4,64,256]{2,1,0:T(8,128)S(1)} collective-permute-done((f32[4,64,256]{2,1,0:T(8,128)S(1)}, f32[4,64,256]{2,1,0:T(8,128)S(1)}, u32[]{:S(2)}, u32[]{:S(2)}) %collective-permute-start.9) | collective-permute-done | bytes 262176 | tf_op jit(solution)/shard_map/ppermute | solution.py:208
  68.6 0.0 collective-permute-done.7
  68.6 0.1 fusion.8
  68.7 0.8 %maximum_select_fusion = f32[2,4,64,256]{3,2,1,0:T(8,128)} fusion(f32[1,4,64,256]{3,2,1,0:T(8,128)S(1)} %fusion.8, f32[1,4,64,256]{3,2,1,0:T(8,128)S(1)} %fusion.12, pred[4,64,256]{2,1,0:T(8,128)(4,1)S(1)} %broadcast_and_fusion), kind=kLoop, calls=%fused_computation.5 | loop fusion | flops 262144 | bytes 1114112 | tf_op jit(solution)/shard_map/jit(_where)/select_n | solution.py:225
  (4 shorter events, 0.1 us)
Async XLA Ops:
  0.0 10.5 %copy-start = (s32[2,256]{1,0:T(2,128)S(1)}, s32[2,256]{1,0:T(2,128)}, u32[]{:S(2)}) copy-start(s32[2,256]{1,0:T(2,128)} %dims_hbm.3) | copy-start | bytes 6148
  7.1 6.4 %collective-permute-start = (f32[2,8,64,256]{3,2,1,0:T(8,128)}, f32[2,8,64,256]{3,2,1,0:T(8,128)}, u32[]{:S(2)}, u32[]{:S(2)}) collective-permute-start(f32[2,8,64,256]{3,2,1,0:T(8,128)} %get-tuple-element.17), channel_id=1, source_target_pairs={{0,64},{64,0},{128,192},{192,128},{1,65},{65,1},{129,193},{193,129... | collective-permute-start | bytes 3145736 | tf_op jit(solution)/shard_map/ppermute | solution.py:192
  10.4 4.5 %collective-permute-start.1 = (f32[2,8,64,256]{3,2,1,0:T(8,128)S(1)}, f32[2,8,64,256]{3,2,1,0:T(8,128)}, u32[]{:S(2)}, u32[]{:S(2)}) collective-permute-start(f32[2,8,64,256]{3,2,1,0:T(8,128)S(1)} %get-tuple-element.19), channel_id=1, source_target_pairs={{0,64},{64,0},{128,192},{192,128},{1,65},{65,1},{129,193},{193,129... | collective-permute-start | bytes 3145736 | tf_op jit(solution)/shard_map/ppermute | solution.py:192
  25.4 19.5 %collective-permute-start.4 = (f32[2,4,64,256]{3,2,1,0:T(8,128)S(1)}, f32[2,4,64,256]{3,2,1,0:T(8,128)S(1)}, u32[]{:S(2)}, u32[]{:S(2)}) collective-permute-start(f32[2,4,64,256]{3,2,1,0:T(8,128)S(1)} %get-tuple-element.28), channel_id=1, source_target_pairs={{1,0},{2,1},{3,2},{4,3},{5,4},{6,5},{7,6},{136,7},{9,8},{10,9},{11... | collective-permute-start | bytes 1572872 | tf_op jit(solution)/shard_map/ppermute | solution.py:205
  34.0 18.2 %collective-permute-start.3 = (f32[2,4,64,256]{3,2,1,0:T(8,128)S(1)}, f32[2,4,64,256]{3,2,1,0:T(8,128)S(1)}, u32[]{:S(2)}, u32[]{:S(2)}) collective-permute-start(f32[2,4,64,256]{3,2,1,0:T(8,128)S(1)} %get-tuple-element.27), channel_id=1, source_target_pairs={{0,1},{1,2},{2,3},{3,4},{4,5},{5,6},{6,7},{7,136},{8,9},{9,10},{10... | collective-permute-start | bytes 1572872 | tf_op jit(solution)/shard_map/ppermute | solution.py:204
  34.0 18.2 %collective-permute-start.2 = (f32[2,4,64,256]{3,2,1,0:T(8,128)S(1)}, f32[2,4,64,256]{3,2,1,0:T(8,128)S(1)}, u32[]{:S(2)}, u32[]{:S(2)}) collective-permute-start(f32[2,4,64,256]{3,2,1,0:T(8,128)S(1)} %get-tuple-element.22), channel_id=1, source_target_pairs={{0,64},{64,0},{128,192},{192,128},{1,65},{65,1},{129,193},{193,129... | collective-permute-start | bytes 1572872 | tf_op jit(solution)/shard_map/ppermute | solution.py:192
  34.7 18.7 %collective-permute-start.8 = (f32[8,64,256]{2,1,0:T(8,128)S(1)}, f32[8,64,256]{2,1,0:T(8,128)S(1)}, u32[]{:S(2)}, u32[]{:S(2)}) collective-permute-start(f32[8,64,256]{2,1,0:T(8,128)S(1)} %fusion.2), channel_id=1, source_target_pairs={{0,128},{64,192},{128,0},{192,64},{1,129},{65,193},{129,1},{193,65... | collective-permute-start | bytes 1572872 | tf_op jit(solution)/shard_map/ppermute | solution.py:195
  35.4 21.3 %collective-permute-start.6 = (f32[2,4,64,256]{3,2,1,0:T(8,128)S(1)}, f32[2,4,64,256]{3,2,1,0:T(8,128)S(1)}, u32[]{:S(2)}, u32[]{:S(2)}) collective-permute-start(f32[2,4,64,256]{3,2,1,0:T(8,128)S(1)} %get-tuple-element.25), channel_id=1, source_target_pairs={{0,64},{64,0},{128,192},{192,128},{1,65},{65,1},{129,193},{193,129... | collective-permute-start | bytes 1572872 | tf_op jit(solution)/shard_map/ppermute | solution.py:192
  52.4 6.4 %collective-permute-start.5 = (f32[4,64,256]{2,1,0:T(8,128)S(1)}, f32[4,64,256]{2,1,0:T(8,128)S(1)}, u32[]{:S(2)}, u32[]{:S(2)}) collective-permute-start(f32[4,64,256]{2,1,0:T(8,128)S(1)} %fusion.9), channel_id=1, source_target_pairs={{0,128},{64,192},{128,0},{192,64},{1,129},{65,193},{129,1},{193,65... | collective-permute-start | bytes 786440 | tf_op jit(solution)/shard_map/ppermute | solution.py:195
  54.6 7.3 %collective-permute-start.10 = (f32[4,64,256]{2,1,0:T(8,128)S(1)}, f32[4,64,256]{2,1,0:T(8,128)S(1)}, u32[]{:S(2)}, u32[]{:S(2)}) collective-permute-start(f32[4,64,256]{2,1,0:T(8,128)S(1)} %get-tuple-element.30), channel_id=1, source_target_pairs={{1,0},{2,1},{3,2},{4,3},{5,4},{6,5},{7,6},{136,7},{9,8},{10,9},{11... | collective-permute-start | bytes 786440 | tf_op jit(solution)/shard_map/ppermute | solution.py:209
  56.7 11.9 %collective-permute-start.9 = (f32[4,64,256]{2,1,0:T(8,128)S(1)}, f32[4,64,256]{2,1,0:T(8,128)S(1)}, u32[]{:S(2)}, u32[]{:S(2)}) collective-permute-start(f32[4,64,256]{2,1,0:T(8,128)S(1)} %get-tuple-element.29), channel_id=1, source_target_pairs={{0,1},{1,2},{2,3},{3,4},{4,5},{5,6},{6,7},{7,136},{8,9},{9,10},{10... | collective-permute-start | bytes 786440 | tf_op jit(solution)/shard_map/ppermute | solution.py:208
  56.7 11.9 %collective-permute-start.7 = (f32[4,64,256]{2,1,0:T(8,128)S(1)}, f32[4,64,256]{2,1,0:T(8,128)S(1)}, u32[]{:S(2)}, u32[]{:S(2)}) collective-permute-start(f32[4,64,256]{2,1,0:T(8,128)S(1)} %fusion.3), channel_id=1, source_target_pairs={{0,128},{64,192},{128,0},{192,64},{1,129},{65,193},{129,1},{193,65... | collective-permute-start | bytes 786440 | tf_op jit(solution)/shard_map/ppermute | solution.py:195

commit v2 on v0

v2 whole, which is shorter than its diff:
```python
import functools

import jax
import jax.numpy as jnp
from jax import lax
from jax.experimental import pallas as pl
from jax.experimental.pallas import tpu as pltpu
from jax.sharding import PartitionSpec as P

Z_RUN = 8
BOTH = ("ops", "sec")
EARLY = 2
NT = (((1,), (1,)), ((), ()))
NN = (((1,), (0,)), ((), ()))


def terms_kernel(
    me_ref, dims_hbm, pair_hbm, wave_ref, left_ref, right_ref,
    keep0, send0, keep1, send1, inside,
    wave_buf, masked, left_buf, right_buf, half, dims_ref, pair_ref,
    wave_sem, left_sem, right_sem, dims_sem, pair_sem,
):
    terms, sectors, pad, _ = left_ref.shape
    run = pad // 4
    peers = dims_ref.shape[1] // sectors
    me = me_ref[0]
    sec, ops = me % peers, me // peers
    core, x_lo = ops % 2, ops // 2
    first = sec * sectors
    z = sec % Z_RUN

    pair_copy = pltpu.make_async_copy(pair_hbm, pair_ref, pair_sem)
    dims_copy = pltpu.make_async_copy(dims_hbm, dims_ref, dims_sem)
    parts = [(0, 0, EARLY), (0, EARLY, terms - EARLY)] + [(l, 0, terms) for l in range(1, sectors)]

    def wave_copy(l):
        return pltpu.make_async_copy(wave_ref.at[:, l], wave_buf.at[:, l], wave_sem.at[l])

    def right_copy(i):
        l, t, number = parts[i]
        at = pl.ds(t, number)
        return pltpu.make_async_copy(right_ref.at[at, l], right_buf.at[l, at], right_sem.at[i])

    def left_copy(i):
        l, t, number = parts[i]
        at = pl.ds(t, number)
        return pltpu.make_async_copy(left_ref.at[at, l], left_buf.at[l, at], left_sem.at[i])

    dims_copy.start()
    pair_copy.start()
    wave_copy(0).start()
    right_copy(0).start()
    left_copy(0).start()
    for i in range(1, len(parts)):
        if i < sectors:
            wave_copy(i).start(priority=1)
        right_copy(i).start(priority=1)
        left_copy(i).start(priority=1)

    for ref in (keep0, send0, keep1, send1):
        ref[...] = jnp.zeros_like(ref)
    rows = lax.broadcasted_iota(jnp.int32, (pad, pad), 0)
    cols = lax.broadcasted_iota(jnp.int32, (pad, pad), 1)

    def mask(l):
        valid = (rows < dims_ref[0, first + l]) & (cols < dims_ref[1, first + l])
        for v in range(2):
            value = jnp.where(valid, wave_buf[v, l].astype(jnp.float32), 0.0)
            masked[l, v * pad : (v + 1) * pad] = value.astype(jnp.bfloat16)

    def first_stage(l, t, u):
        product = lax.dot_general(masked[l], right_buf[l, t], NT, preferred_element_type=jnp.float32)
        half[u] = product.astype(jnp.bfloat16)

    def second_stage(l, t, u):
        place = pair_ref[l, t] - first
        flip = ((place < 0) & (z == 0)) | ((place >= sectors) & (z == Z_RUN - 1))
        near = x_lo ^ flip.astype(jnp.int32)
        blocks = [2 * near + core, 2 * (1 - near) + core, 2 * near + 1 - core, 2 * (1 - near) + 1 - core]
        lhs = jnp.concatenate(
            [left_buf[l, t, pl.ds(pl.multiple_of(b * run, run), run), :] for b in blocks], axis=0
        )
        for v, (keep, send) in enumerate(((keep0, send0), (keep1, send1))):
            term = lax.dot_general(lhs, half[u, v * pad : (v + 1) * pad], NN, preferred_element_type=jnp.float32)
            for q in range(2):
                keep[place + sectors, q] += term[q * run : (q + 1) * run]
                send[place + sectors, q] += term[(2 + q) * run : (3 + q) * run]

    dims_copy.wait()
    own_rows = lax.broadcasted_iota(jnp.int32, (run, pad), 0) + ops * run
    own_cols = lax.broadcasted_iota(jnp.int32, (run, pad), 1)
    for l in range(sectors):
        valid = (own_rows < dims_ref[0, first + l]) & (own_cols < dims_ref[1, first + l])
        inside[l] = jnp.where(valid, 1.0, 0.0)
    pair_copy.wait()
    for i, (l, t, number) in enumerate(parts):
        if t == 0:
            wave_copy(l).wait()
        right_copy(i).wait()
        left_copy(i).wait()
        if t == 0:
            mask(l)
        first_stage(l, t, 0)
        for u in range(number):
            if u + 1 < number:
                first_stage(l, t + u + 1, u + 1)
            second_stage(l, t + u, u)


def terms_call(me, dims, pairing, wave, left, right):
    terms, sectors, pad, _ = left.shape
    pairs = terms * sectors
    shape = jax.ShapeDtypeStruct((3 * sectors, 2, pad // 4, pad), jnp.float32)
    in_hbm = pl.BlockSpec(memory_space=pltpu.HBM)
    vmem = pl.BlockSpec(memory_space=pltpu.VMEM)
    operands = (dims, pairing.T, wave, left, right)
    return pl.pallas_call(
        terms_kernel,
        out_shape=(shape,) * 4 + (jax.ShapeDtypeStruct((sectors, pad // 4, pad), jnp.float32),),
        in_specs=[pl.BlockSpec(memory_space=pltpu.SMEM)] + [in_hbm] * 5,
        out_specs=(vmem,) * 5,
        scratch_shapes=[
            pltpu.VMEM(wave.shape, jnp.bfloat16),
            pltpu.VMEM((sectors, 2 * pad, pad), jnp.bfloat16),
            pltpu.VMEM((sectors, terms, pad, pad), jnp.bfloat16),
            pltpu.VMEM((sectors, terms, pad, pad), jnp.bfloat16),
            pltpu.VMEM((terms, 2 * pad, pad), jnp.bfloat16),
            pltpu.SMEM(dims.shape, jnp.int32),
            pltpu.SMEM((sectors, terms), jnp.int32),
            pltpu.SemaphoreType.DMA((sectors,)),
            pltpu.SemaphoreType.DMA((sectors + 1,)),
            pltpu.SemaphoreType.DMA((sectors + 1,)),
            pltpu.SemaphoreType.DMA,
            pltpu.SemaphoreType.DMA,
        ],
        compiler_params=pltpu.CompilerParams(vmem_limit_bytes=32 * 1024 * 1024),
        cost_estimate=pl.CostEstimate(
            flops=pairs * 8 * pad**3, bytes_accessed=pairs * pad * pad * 4, transcendentals=0
        ),
        name="terms",
    )(me.reshape(1), *(pltpu.with_memory_space_constraint(x, pltpu.HBM) for x in operands))


def small_call(kernel, name, out_shapes, *args):
    shapes = tuple(jax.ShapeDtypeStruct(s, jnp.float32) for s in out_shapes)
    size = sum(4 * x.size for x in args)
    vmem = pl.BlockSpec(memory_space=pltpu.VMEM)
    result = pl.pallas_call(
        kernel,
        out_shape=shapes,
        in_specs=[vmem] * len(args),
        out_specs=(vmem,) * len(shapes),
        compiler_params=pltpu.CompilerParams(vmem_limit_bytes=8 * 1024 * 1024),
        cost_estimate=pl.CostEstimate(flops=size // 4, bytes_accessed=size, transcendentals=0),
        name=name,
    )(*args)
    return result if len(shapes) > 1 else result[0]


def split_kernel(keep, got, down, up):
    sectors = down.shape[0]
    down[...] = keep[:sectors] + got[:sectors]
    up[...] = keep[2 * sectors :] + got[2 * sectors :]


def far_kernel(keep, got, halo, own):
    sectors = own.shape[0]
    halo[:sectors] = keep[:sectors, 1] + got[:sectors, 1]
    halo[sectors:] = keep[2 * sectors :, 1] + got[2 * sectors :, 1]
    own[...] = keep[sectors : 2 * sectors, 1] + got[sectors : 2 * sectors, 1]


def near_kernel(keep, got, far, down, up):
    sectors = down.shape[0]
    down[...] = keep[:sectors, 0] + got[:sectors, 0] + far[:sectors]
    up[...] = keep[2 * sectors :, 0] + got[2 * sectors :, 0] + far[sectors:]


def add_kernel(a, b, out):
    out[...] = a[...] + b[...]


def own_far_kernel(keep, got, both, out):
    sectors = out.shape[0]
    out[...] = keep[sectors : 2 * sectors, 1] + got[sectors : 2 * sectors, 1] + both[:, 1]


def finish_kernel(keep0, got0, both0, far0, keep1, got1, own_far1, below1, above1, inside, out):
    sectors = out.shape[1]
    for l in range(sectors):
        s = sectors + l
        valid = inside[l] > 0.0
        out[0, l] = jnp.where(valid, keep0[s, 0] + got0[s, 0] + both0[l, 0] + far0[l], 0.0)
        out[1, l] = jnp.where(valid, keep1[s, 0] + got1[s, 0] + own_far1[l] + below1[l] + above1[l], 0.0)


def body(wavefunction, left_blocks, right_blocks, pairing, sector_dims):
    sectors, pad = wavefunction.shape[1:3]
    run = pad // 4
    peers = lax.axis_size("sec")
    other_core = [(i, i ^ 1) for i in range(4)]
    other_chip = [(i, i ^ 2) for i in range(4)]
    upward = [
        (o * peers + s, (o ^ 2 if s % Z_RUN == Z_RUN - 1 else o) * peers + (s + 1) % peers)
        for o in range(4)
        for s in range(peers)
    ]
    downward = [(b, a) for a, b in upward]
    near, both = (sectors, run, pad), (sectors, 2, run, pad)

    def to_core(x):
        return lax.ppermute(x, "ops", other_core)

    def to_chip(x):
        return lax.ppermute(x, "ops", other_chip)

    def to_sector(down, up):
        return lax.ppermute(up, BOTH, upward), lax.ppermute(down, BOTH, downward)

    keep0, send0, keep1, send1, inside = terms_call(
        lax.axis_index(BOTH), sector_dims, pairing, wavefunction, left_blocks, right_blocks
    )
    got1 = to_core(send1)
    got0 = to_core(send0)
    far1, own_far1 = small_call(far_kernel, "far1", ((2 * sectors, run, pad), near), keep1, got1)
    got0, far1 = lax.optimization_barrier((got0, far1))
    far1 = to_chip(far1)
    down0, up0 = small_call(split_kernel, "split0", (both, both), keep0, got0)
    below0, above0 = to_sector(down0, up0)
    far1, own_far1 = lax.optimization_barrier((far1, own_far1))
    down1, up1 = small_call(near_kernel, "near1", (near, near), keep1, got1, far1)
    below1, above1 = to_sector(down1, up1)
    own_far1 = to_chip(own_far1)
    both0 = small_call(add_kernel, "both0", (both,), below0, above0)
    far0 = to_chip(small_call(own_far_kernel, "own_far0", (near,), keep0, got0, both0))
    return small_call(
        finish_kernel, "finish", ((2, sectors, run, pad),),
        keep0, got0, both0, far0, keep1, got1, own_far1, below1, above1, inside,
    )


def solution(mesh):
    placed = (
        P(None, "sec", None, None),
        P("ops", "sec", None, None),
        P("ops", "sec", None, None),
        P("ops", "sec"),
        P(),
    )
    return jax.shard_map(
        body, mesh=mesh, in_specs=placed, out_specs=P(None, "sec", "ops", None), check_vma=False
    )
```

time: 189 us -> 47.7 us (0.25)
  waiting for transfers between devices: 83.3 us -> 14.7 us
  local copies, waits for them, and re-layouts: 41.9 us -> 0 us
  matrix products: 39.3 us -> 0 us
  starting transfers between devices: 5.8 us -> 22.2 us
  between operations: 13.5 us -> 0.04 us
  Pallas kernels: 0 us -> 10.5 us
  other arithmetic: 3.89 us -> 0 us
    dot_general x3 -> x0, matrix products: 39.3 us -> none  [the longest x1 16.9 us: body(): jnp.einsum('tls,vtlab->vsab', onehot, term_contribution, precision=lax.Pr...]
    unnamed x2 -> x0, waiting for transfers between devices: 36.4 us -> none
    transpose x1 -> x0, local copies, waits for them, and re-layouts: 32.7 us -> none  [body(): jnp.einsum('tlac,vtlcb->vtlab', left_blocks, partial_product, preferred_e...]
    ppermute x2 -> x9, waiting for transfers between devices: 46.9 us -> 14.7 us  [the longest x2 5.1 us: to_core(): return lax.ppermute(x, 'ops', other_core)]
    ppermute x2 -> x9, starting transfers between devices: 5.79 us -> 22.2 us  [the longest x4 18.1 us: to_sector(): return (lax.ppermute(up, BOTH, upward), lax.ppermute(down, BOTH, downward))]
    pallas_call x0 -> x7, Pallas kernels: none -> 10.5 us  [the longest x1 9.18 us: terms_call(): pl.pallas_call(terms_kernel, out_shape=(shape,) * 4 + (jax.ShapeDtypeStru...]
    unnamed x8 -> x0, local copies, waits for them, and re-layouts: 4.21 us -> none
    slice x1 -> x0, local copies, waits for them, and re-layouts: 4.01 us -> none  [body(): from_below = shifted(spread[:, 2 * sector_per_device:], 'sec', 1)]
  transfers between devices with their start and end apart: 3 -> 9, of which waited for: 3 -> 5; matrix products, arithmetic and copies ran while one was open for 0% -> 0% of each run, Pallas kernels for 0% -> 1%
where the time goes in v2:
time: 47.7 us; the launch traced here: 47.4 us
  starting transfers between devices  22.2 us (47%)
  waiting for transfers between devices  14.7 us (31%)
  Pallas kernels  10.5 us (22%)
    ppermute x4, starting transfers between devices, to_sector(): return (lax.ppermute(up, BOTH, upward), lax.ppermute(down, BOTH, downward))  18.1 us
    pallas_call x1, Pallas kernels, terms_call(): pl.pallas_call(terms_kernel, out_shape=(shape,) * 4 + (jax.ShapeDtypeStru...  9.18 us
    ppermute x2, waiting for transfers between devices, to_core(): return lax.ppermute(x, 'ops', other_core)  5.1 us
    ppermute x3, waiting for transfers between devices, to_chip(): return lax.ppermute(x, 'ops', other_chip)  5.02 us
    ppermute x4, waiting for transfers between devices, to_sector(): return (lax.ppermute(up, BOTH, upward), lax.ppermute(down, BOTH, downward))  4.54 us
    ppermute x2, starting transfers between devices, to_core(): return lax.ppermute(x, 'ops', other_core)  3.42 us
    pallas_call x6, Pallas kernels, small_call(): pl.pallas_call(kernel, out_shape=shapes, in_specs=[vmem] * len(args), out...  1.3 us
  transfers between devices with their start and end apart: 9, of which 5 were waited for; matrix products, arithmetic and copies ran while one was open for 0% of the time, Pallas kernels for 1%

profile of v2, /device:TPU:1, one launch (start us, length us, event | category | flops | bytes accessed | tf_op | source)
XLA Modules:
  0.0 47.4 jit_solution(3125737221355074170)
XLA Ops:
  0.0 9.2 %terms.1 = (f32[12,2,64,256]{3,2,1,0:T(8,128)S(1)}, f32[12,2,64,256]{3,2,1,0:T(8,128)S(1)}, f32[12,2,64,256]{3,2,1,0:T(8,128)S(1)}, f32[12,2,64,256]{3,2,1,0:T(8,128)S(1)}, f32[4,64,256]{2,1,0:T(8,128)S(1)}) custom-call(s32[1]{0:T(128)} %bitcast.me_ref, s32[2,256]{1,0:T(2,128)} %dims_hbm.1, s32[4,10]{1,0:T(4,128)} %bitcast.2, ...), custom_call_target="tpu_custom_call" | custom-call | flops 5368709120 | bytes 10485760 | tf_op jit(solution)/shard_map/terms/pallas_call | solution.py:117
  9.2 3.3 %collective-permute-start.1 = (f32[12,2,64,256]{3,2,1,0:T(8,128)S(1)}, f32[12,2,64,256]{3,2,1,0:T(8,128)S(1)}, u32[]{:S(2)}, u32[]{:S(2)}) collective-permute-start(f32[12,2,64,256]{3,2,1,0:T(8,128)S(1)} %get-tuple-element.23), channel_id=1, source_target_pairs={{0,64},{64,0},{128,192},{192,128},{1,65},{65,1},{129,193},{193,129... | collective-permute-start | bytes 4718600 | tf_op jit(solution)/shard_map/ppermute | solution.py:212
  12.5 0.1 collective-permute-start
  12.6 2.9 %collective-permute-done.1.got.got1 = f32[12,2,64,256]{3,2,1,0:T(8,128)S(1)} collective-permute-done((f32[12,2,64,256]{3,2,1,0:T(8,128)S(1)}, f32[12,2,64,256]{3,2,1,0:T(8,128)S(1)}, u32[]{:S(2)}, u32[]{:S(2)}) %collective-permute-start.1) | collective-permute-done | bytes 1572896 | tf_op jit(solution)/shard_map/ppermute | solution.py:212
  15.5 0.1 far1.1
  15.6 2.2 %collective-permute-done.got.got0 = f32[12,2,64,256]{3,2,1,0:T(8,128)S(1)} collective-permute-done((f32[12,2,64,256]{3,2,1,0:T(8,128)S(1)}, f32[12,2,64,256]{3,2,1,0:T(8,128)S(1)}, u32[]{:S(2)}, u32[]{:S(2)}) %collective-permute-start) | collective-permute-done | bytes 1572896 | tf_op jit(solution)/shard_map/ppermute | solution.py:212
  17.8 0.0 collective-permute-start.5
  17.8 0.1 split0.1
  17.9 1.2 %collective-permute-start.2 = (f32[4,2,64,256]{3,2,1,0:T(8,128)S(1)}, f32[4,2,64,256]{3,2,1,0:T(8,128)S(1)}, u32[]{:S(2)}, u32[]{:S(2)}) collective-permute-start(f32[4,2,64,256]{3,2,1,0:T(8,128)S(1)} %get-tuple-element.26), channel_id=1, source_target_pairs={{0,1},{1,2},{2,3},{3,4},{4,5},{5,6},{6,7},{7,136},{8,9},{9,10},{10... | collective-permute-start | bytes 1572872 | tf_op jit(solution)/shard_map/ppermute | solution.py:218
  19.1 8.0 %collective-permute-start.3 = (f32[4,2,64,256]{3,2,1,0:T(8,128)S(1)}, f32[4,2,64,256]{3,2,1,0:T(8,128)S(1)}, u32[]{:S(2)}, u32[]{:S(2)}) collective-permute-start(f32[4,2,64,256]{3,2,1,0:T(8,128)S(1)} %get-tuple-element.27), channel_id=1, source_target_pairs={{1,0},{2,1},{3,2},{4,3},{5,4},{6,5},{7,6},{136,7},{9,8},{10,9},{11... | collective-permute-start | bytes 1572872 | tf_op jit(solution)/shard_map/ppermute | solution.py:218
  27.1 3.8 %collective-permute-done.5.far = f32[8,64,256]{2,1,0:T(8,128)S(1)} collective-permute-done((f32[8,64,256]{2,1,0:T(8,128)S(1)}, f32[8,64,256]{2,1,0:T(8,128)S(1)}, u32[]{:S(2)}, u32[]{:S(2)}) %collective-permute-start.5) | collective-permute-done | bytes 524320 | tf_op jit(solution)/shard_map/ppermute | solution.py:215
  30.9 0.3 collective-permute-start.6
  31.3 0.1 near1.1
  31.3 0.9 %collective-permute-start.7 = (f32[4,64,256]{2,1,0:T(8,128)S(1)}, f32[4,64,256]{2,1,0:T(8,128)S(1)}, u32[]{:S(2)}, u32[]{:S(2)}) collective-permute-start(f32[4,64,256]{2,1,0:T(8,128)S(1)} %get-tuple-element.32), channel_id=1, source_target_pairs={{0,1},{1,2},{2,3},{3,4},{4,5},{5,6},{6,7},{7,136},{8,9},{9,10},{10... | collective-permute-start | bytes 786440 | tf_op jit(solution)/shard_map/ppermute | solution.py:218
  32.2 8.0 %collective-permute-start.8 = (f32[4,64,256]{2,1,0:T(8,128)S(1)}, f32[4,64,256]{2,1,0:T(8,128)S(1)}, u32[]{:S(2)}, u32[]{:S(2)}) collective-permute-start(f32[4,64,256]{2,1,0:T(8,128)S(1)} %get-tuple-element.33), channel_id=1, source_target_pairs={{1,0},{2,1},{3,2},{4,3},{5,4},{6,5},{7,6},{136,7},{9,8},{10,9},{11... | collective-permute-start | bytes 786440 | tf_op jit(solution)/shard_map/ppermute | solution.py:218
  40.2 0.0 collective-permute-done.2.a
  40.2 0.0 collective-permute-done.3.b
  40.2 0.1 both0.1.both
  40.3 0.4 collective-permute-start.4
  40.7 0.0 collective-permute-done.6.own_far1
  40.7 4.5 %collective-permute-done.7.below1 = f32[4,64,256]{2,1,0:T(8,128)S(1)} collective-permute-done((f32[4,64,256]{2,1,0:T(8,128)S(1)}, f32[4,64,256]{2,1,0:T(8,128)S(1)}, u32[]{:S(2)}, u32[]{:S(2)}) %collective-permute-start.7) | collective-permute-done | bytes 262176 | tf_op jit(solution)/shard_map/ppermute | solution.py:218
  45.3 0.0 collective-permute-done.8.above1
  45.3 1.2 %collective-permute-done.4.far0 = f32[4,64,256]{2,1,0:T(8,128)S(1)} collective-permute-done((f32[4,64,256]{2,1,0:T(8,128)S(1)}, f32[4,64,256]{2,1,0:T(8,128)S(1)}, u32[]{:S(2)}, u32[]{:S(2)}) %collective-permute-start.4) | collective-permute-done | bytes 262176 | tf_op jit(solution)/shard_map/ppermute | solution.py:215
  46.5 0.9 %finish.1 = f32[2,4,64,256]{3,2,1,0:T(8,128)} custom-call(f32[12,2,64,256]{3,2,1,0:T(8,128)S(1)} %get-tuple-element.20.keep.keep0, f32[12,2,64,256]{3,2,1,0:T(8,128)S(1)} %collective-permute-done.got.got0, f32[4,2,64,256]{3,2,1,0:T(8,128)S(1)} %both0.1.both, f32[4,64,256]{2,1,0:T(8,128)S(1)} %collective-permute-done.4.far0, ...), custom_call_target="tpu_custom_call" | custom-call | flops 2031616 | bytes 8126464 | tf_op jit(solution)/shard_map/finish/pallas_call | solution.py:148
  (1 shorter events, 0.0 us)
Async XLA Ops:
  9.2 6.4 %collective-permute-start.1 = (f32[12,2,64,256]{3,2,1,0:T(8,128)S(1)}, f32[12,2,64,256]{3,2,1,0:T(8,128)S(1)}, u32[]{:S(2)}, u32[]{:S(2)}) collective-permute-start(f32[12,2,64,256]{3,2,1,0:T(8,128)S(1)} %get-tuple-element.23), channel_id=1, source_target_pairs={{0,64},{64,0},{128,192},{192,128},{1,65},{65,1},{129,193},{193,129... | collective-permute-start | bytes 4718600 | tf_op jit(solution)/shard_map/ppermute | solution.py:212
  12.5 5.3 %collective-permute-start = (f32[12,2,64,256]{3,2,1,0:T(8,128)S(1)}, f32[12,2,64,256]{3,2,1,0:T(8,128)S(1)}, u32[]{:S(2)}, u32[]{:S(2)}) collective-permute-start(f32[12,2,64,256]{3,2,1,0:T(8,128)S(1)} %get-tuple-element.21), channel_id=1, source_target_pairs={{0,64},{64,0},{128,192},{192,128},{1,65},{65,1},{129,193},{193,129... | collective-permute-start | bytes 4718600 | tf_op jit(solution)/shard_map/ppermute | solution.py:212
  17.8 13.1 %collective-permute-start.5 = (f32[8,64,256]{2,1,0:T(8,128)S(1)}, f32[8,64,256]{2,1,0:T(8,128)S(1)}, u32[]{:S(2)}, u32[]{:S(2)}) collective-permute-start(f32[8,64,256]{2,1,0:T(8,128)S(1)} %get-tuple-element.28), channel_id=1, source_target_pairs={{0,128},{64,192},{128,0},{192,64},{1,129},{65,193},{129,1},{193,65... | collective-permute-start | bytes 1572872 | tf_op jit(solution)/shard_map/ppermute | solution.py:215
  17.9 22.3 %collective-permute-start.2 = (f32[4,2,64,256]{3,2,1,0:T(8,128)S(1)}, f32[4,2,64,256]{3,2,1,0:T(8,128)S(1)}, u32[]{:S(2)}, u32[]{:S(2)}) collective-permute-start(f32[4,2,64,256]{3,2,1,0:T(8,128)S(1)} %get-tuple-element.26), channel_id=1, source_target_pairs={{0,1},{1,2},{2,3},{3,4},{4,5},{5,6},{6,7},{7,136},{8,9},{9,10},{10... | collective-permute-start | bytes 1572872 | tf_op jit(solution)/shard_map/ppermute | solution.py:218
  19.1 21.1 %collective-permute-start.3 = (f32[4,2,64,256]{3,2,1,0:T(8,128)S(1)}, f32[4,2,64,256]{3,2,1,0:T(8,128)S(1)}, u32[]{:S(2)}, u32[]{:S(2)}) collective-permute-start(f32[4,2,64,256]{3,2,1,0:T(8,128)S(1)} %get-tuple-element.27), channel_id=1, source_target_pairs={{1,0},{2,1},{3,2},{4,3},{5,4},{6,5},{7,6},{136,7},{9,8},{10,9},{11... | collective-permute-start | bytes 1572872 | tf_op jit(solution)/shard_map/ppermute | solution.py:218
  30.9 9.8 %collective-permute-start.6 = (f32[4,64,256]{2,1,0:T(8,128)S(1)}, f32[4,64,256]{2,1,0:T(8,128)S(1)}, u32[]{:S(2)}, u32[]{:S(2)}) collective-permute-start(f32[4,64,256]{2,1,0:T(8,128)S(1)} %get-tuple-element.30), channel_id=1, source_target_pairs={{0,128},{64,192},{128,0},{192,64},{1,129},{65,193},{129,1},{193,65... | collective-permute-start | bytes 786440 | tf_op jit(solution)/shard_map/ppermute | solution.py:215
  31.3 13.9 %collective-permute-start.7 = (f32[4,64,256]{2,1,0:T(8,128)S(1)}, f32[4,64,256]{2,1,0:T(8,128)S(1)}, u32[]{:S(2)}, u32[]{:S(2)}) collective-permute-start(f32[4,64,256]{2,1,0:T(8,128)S(1)} %get-tuple-element.32), channel_id=1, source_target_pairs={{0,1},{1,2},{2,3},{3,4},{4,5},{5,6},{6,7},{7,136},{8,9},{9,10},{10... | collective-permute-start | bytes 786440 | tf_op jit(solution)/shard_map/ppermute | solution.py:218
  32.2 13.1 %collective-permute-start.8 = (f32[4,64,256]{2,1,0:T(8,128)S(1)}, f32[4,64,256]{2,1,0:T(8,128)S(1)}, u32[]{:S(2)}, u32[]{:S(2)}) collective-permute-start(f32[4,64,256]{2,1,0:T(8,128)S(1)} %get-tuple-element.33), channel_id=1, source_target_pairs={{1,0},{2,1},{3,2},{4,3},{5,4},{6,5},{7,6},{136,7},{9,8},{10,9},{11... | collective-permute-start | bytes 786440 | tf_op jit(solution)/shard_map/ppermute | solution.py:218
  40.3 6.1 %collective-permute-start.4 = (f32[4,64,256]{2,1,0:T(8,128)S(1)}, f32[4,64,256]{2,1,0:T(8,128)S(1)}, u32[]{:S(2)}, u32[]{:S(2)}) collective-permute-start(f32[4,64,256]{2,1,0:T(8,128)S(1)} %own_far0.1), channel_id=1, source_target_pairs={{0,128},{64,192},{128,0},{192,64},{1,129},{65,193},{129,1},{193,65... | collective-permute-start | bytes 786440 | tf_op jit(solution)/shard_map/ppermute | solution.py:215

commit v3 on v2

--- a/solution.py
+++ b/solution.py
@@ -9,6 +9,7 @@
 
 Z_RUN = 8
 BOTH = ("ops", "sec")
+WEIGHTY = ("base0", "base1", "sum1", "up1")
 EARLY = 2
 NT = (((1,), (1,)), ((), ()))
 NN = (((1,), (0,)), ((), ()))
@@ -16,8 +17,8 @@
 
 def terms_kernel(
     me_ref, dims_hbm, pair_hbm, wave_ref, left_ref, right_ref,
-    keep0, send0, keep1, send1, inside,
-    wave_buf, masked, left_buf, right_buf, half, dims_ref, pair_ref,
+    keep0, keep1, send0, send1, send_own, inside,
+    wave_buf, masked, left_buf, right_buf, half, sums, dims_ref, pair_ref,
     wave_sem, left_sem, right_sem, dims_sem, pair_sem,
 ):
     terms, sectors, pad, _ = left_ref.shape
@@ -57,7 +58,7 @@
         right_copy(i).start(priority=1)
         left_copy(i).start(priority=1)
 
-    for ref in (keep0, send0, keep1, send1):
+    for ref in (keep0, keep1, sums):
         ref[...] = jnp.zeros_like(ref)
     rows = lax.broadcasted_iota(jnp.int32, (pad, pad), 0)
     cols = lax.broadcasted_iota(jnp.int32, (pad, pad), 1)
@@ -80,11 +81,11 @@
         lhs = jnp.concatenate(
             [left_buf[l, t, pl.ds(pl.multiple_of(b * run, run), run), :] for b in blocks], axis=0
         )
-        for v, (keep, send) in enumerate(((keep0, send0), (keep1, send1))):
+        for v, keep in enumerate((keep0, keep1)):
             term = lax.dot_general(lhs, half[u, v * pad : (v + 1) * pad], NN, preferred_element_type=jnp.float32)
             for q in range(2):
                 keep[place + sectors, q] += term[q * run : (q + 1) * run]
-                send[place + sectors, q] += term[(2 + q) * run : (3 + q) * run]
+                sums[v, place + sectors, q] += term[(2 + q) * run : (3 + q) * run]
 
     dims_copy.wait()
     own_rows = lax.broadcasted_iota(jnp.int32, (run, pad), 0) + ops * run
@@ -105,26 +106,36 @@
             if u + 1 < number:
                 first_stage(l, t + u + 1, u + 1)
             second_stage(l, t + u, u)
+    for v, send in enumerate((send0, send1)):
+        send[:sectors] = sums[v, :sectors]
+        send[sectors:] = sums[v, 2 * sectors :]
+    send_own[...] = sums[:, sectors : 2 * sectors]
 
 
 def terms_call(me, dims, pairing, wave, left, right):
     terms, sectors, pad, _ = left.shape
     pairs = terms * sectors
-    shape = jax.ShapeDtypeStruct((3 * sectors, 2, pad // 4, pad), jnp.float32)
+    def shape(*leading):
+        return jax.ShapeDtypeStruct((*leading, pad // 4, pad), jnp.float32)
+
     in_hbm = pl.BlockSpec(memory_space=pltpu.HBM)
     vmem = pl.BlockSpec(memory_space=pltpu.VMEM)
     operands = (dims, pairing.T, wave, left, right)
     return pl.pallas_call(
         terms_kernel,
-        out_shape=(shape,) * 4 + (jax.ShapeDtypeStruct((sectors, pad // 4, pad), jnp.float32),),
+        out_shape=(
+            shape(3 * sectors, 2), shape(3 * sectors, 2), shape(2 * sectors, 2), shape(2 * sectors, 2),
+            shape(2, sectors, 2), shape(sectors),
+        ),
         in_specs=[pl.BlockSpec(memory_space=pltpu.SMEM)] + [in_hbm] * 5,
-        out_specs=(vmem,) * 5,
+        out_specs=(vmem,) * 6,
         scratch_shapes=[
             pltpu.VMEM(wave.shape, jnp.bfloat16),
             pltpu.VMEM((sectors, 2 * pad, pad), jnp.bfloat16),
             pltpu.VMEM((sectors, terms, pad, pad), jnp.bfloat16),
             pltpu.VMEM((sectors, terms, pad, pad), jnp.bfloat16),
             pltpu.VMEM((terms, 2 * pad, pad), jnp.bfloat16),
+            pltpu.VMEM((2, 3 * sectors, 2, pad // 4, pad), jnp.float32),
             pltpu.SMEM(dims.shape, jnp.int32),
             pltpu.SMEM((sectors, terms), jnp.int32),
             pltpu.SemaphoreType.DMA((sectors,)),
@@ -143,7 +154,7 @@
 
 def small_call(kernel, name, out_shapes, *args):
     shapes = tuple(jax.ShapeDtypeStruct(s, jnp.float32) for s in out_shapes)
-    size = sum(4 * x.size for x in args)
+    size = (40 if name in WEIGHTY else 1) * sum(4 * x.size for x in args)
     vmem = pl.BlockSpec(memory_space=pltpu.VMEM)
     result = pl.pallas_call(
         kernel,
@@ -157,41 +168,60 @@
     return result if len(shapes) > 1 else result[0]
 
 
-def split_kernel(keep, got, down, up):
-    sectors = down.shape[0]
-    down[...] = keep[:sectors] + got[:sectors]
-    up[...] = keep[2 * sectors :] + got[2 * sectors :]
-
-
-def far_kernel(keep, got, halo, own):
-    sectors = own.shape[0]
-    halo[:sectors] = keep[:sectors, 1] + got[:sectors, 1]
-    halo[sectors:] = keep[2 * sectors :, 1] + got[2 * sectors :, 1]
-    own[...] = keep[sectors : 2 * sectors, 1] + got[sectors : 2 * sectors, 1]
-
-
-def near_kernel(keep, got, far, down, up):
-    sectors = down.shape[0]
-    down[...] = keep[:sectors, 0] + got[:sectors, 0] + far[:sectors]
-    up[...] = keep[2 * sectors :, 0] + got[2 * sectors :, 0] + far[sectors:]
-
-
-def add_kernel(a, b, out):
-    out[...] = a[...] + b[...]
-
-
-def own_far_kernel(keep, got, both, out):
-    sectors = out.shape[0]
-    out[...] = keep[sectors : 2 * sectors, 1] + got[sectors : 2 * sectors, 1] + both[:, 1]
-
-
-def finish_kernel(keep0, got0, both0, far0, keep1, got1, own_far1, below1, above1, inside, out):
-    sectors = out.shape[1]
-    for l in range(sectors):
-        s = sectors + l
+def up_kernel(keep, got, out):
+    sectors = out.shape[0]
+    out[...] = keep[2 * sectors :] + got[sectors:]
+
+
+def down_kernel(keep, got, out):
+    sectors = out.shape[0]
+    out[...] = keep[:sectors] + got[:sectors]
+
+
+def far_kernel(keep, got, out):
+    sectors = out.shape[0] // 2
+    out[:sectors] = keep[:sectors, 1] + got[:sectors, 1]
+    out[sectors:] = keep[2 * sectors :, 1] + got[sectors:, 1]
+
+
+def near_up_kernel(keep, got, far, out):
+    sectors = out.shape[0]
+    out[...] = keep[2 * sectors :, 0] + got[sectors:, 0] + far[sectors:]
+
+
+def near_down_kernel(keep, got, far, out):
+    sectors = out.shape[0]
+    out[...] = keep[:sectors, 0] + got[:sectors, 0] + far[:sectors]
+
+
+def own_far1_kernel(keep, got, out):
+    sectors = out.shape[0]
+    out[...] = keep[sectors : 2 * sectors, 1] + got[1, :, 1]
+
+
+def base0_kernel(keep, got, below, out):
+    sectors = out.shape[0]
+    out[...] = keep[sectors : 2 * sectors] + got[0] + below[...]
+
+
+def own_far0_kernel(base, above, out):
+    out[...] = base[:, 1] + above[:, 1]
+
+
+def base1_kernel(keep, got, far, below, out):
+    sectors = out.shape[0]
+    out[...] = keep[sectors : 2 * sectors, 0] + got[1, :, 0] + far[...] + below[...]
+
+
+def sum1_kernel(base, above, out):
+    out[...] = base[...] + above[...]
+
+
+def finish_kernel(base0, above0, far0, base1, inside, out):
+    for l in range(out.shape[1]):
         valid = inside[l] > 0.0
-        out[0, l] = jnp.where(valid, keep0[s, 0] + got0[s, 0] + both0[l, 0] + far0[l], 0.0)
-        out[1, l] = jnp.where(valid, keep1[s, 0] + got1[s, 0] + own_far1[l] + below1[l] + above1[l], 0.0)
+        out[0, l] = jnp.where(valid, base0[l, 0] + above0[l, 0] + far0[l], 0.0)
+        out[1, l] = jnp.where(valid, base1[l], 0.0)
 
 
 def body(wavefunction, left_blocks, right_blocks, pairing, sector_dims):
@@ -214,29 +244,40 @@
     def to_chip(x):
         return lax.ppermute(x, "ops", other_chip)
 
-    def to_sector(down, up):
-        return lax.ppermute(up, BOTH, upward), lax.ppermute(down, BOTH, downward)
-
-    keep0, send0, keep1, send1, inside = terms_call(
+    def to_above(x):
+        return lax.ppermute(x, BOTH, upward)
+
+    def to_below(x):
+        return lax.ppermute(x, BOTH, downward)
+
+    def after(first, second):
+        return lax.optimization_barrier((first, second))
+
+    keep0, keep1, send0, send1, send_own, inside = terms_call(
         lax.axis_index(BOTH), sector_dims, pairing, wavefunction, left_blocks, right_blocks
     )
     got1 = to_core(send1)
+    got = to_core(send_own)
+
+    far1 = small_call(far_kernel, "far1", ((2 * sectors, run, pad),), keep1, got1)
+    far1, send0 = after(far1, send0)
     got0 = to_core(send0)
-    far1, own_far1 = small_call(far_kernel, "far1", ((2 * sectors, run, pad), near), keep1, got1)
-    got0, far1 = lax.optimization_barrier((got0, far1))
     far1 = to_chip(far1)
-    down0, up0 = small_call(split_kernel, "split0", (both, both), keep0, got0)
-    below0, above0 = to_sector(down0, up0)
-    far1, own_far1 = lax.optimization_barrier((far1, own_far1))
-    down1, up1 = small_call(near_kernel, "near1", (near, near), keep1, got1, far1)
-    below1, above1 = to_sector(down1, up1)
+    below0 = to_above(small_call(up_kernel, "up0", (both,), keep0, got0))
+    above0 = to_below(small_call(down_kernel, "down0", (both,), keep0, got0))
+
+    below1 = to_above(small_call(near_up_kernel, "up1", (near,), keep1, got1, far1))
+    far1_later, got_later = after(far1, got)
+    own_far1 = small_call(own_far1_kernel, "own_far1", (near,), keep1, got_later)
+    base0 = small_call(base0_kernel, "base0", (both,), keep0, got, below0)
+    far0 = small_call(own_far0_kernel, "own_far0", (near,), base0, above0)
+    own_far1, far1_later = after(own_far1, far1)
+    above1 = to_below(small_call(near_down_kernel, "down1", (near,), keep1, got1, far1_later))
     own_far1 = to_chip(own_far1)
-    both0 = small_call(add_kernel, "both0", (both,), below0, above0)
-    far0 = to_chip(small_call(own_far_kernel, "own_far0", (near,), keep0, got0, both0))
-    return small_call(
-        finish_kernel, "finish", ((2, sectors, run, pad),),
-        keep0, got0, both0, far0, keep1, got1, own_far1, below1, above1, inside,
-    )
+    far0 = to_chip(far0)
+    base1 = small_call(base1_kernel, "base1", (near,), keep1, got, own_far1, below1)
+    sum1 = small_call(sum1_kernel, "sum1", (near,), base1, above1)
+    return small_call(finish_kernel, "finish", ((2, sectors, run, pad),), base0, above0, far0, sum1, inside)
 
 
 def solution(mesh):

time: 47.7 us -> 45.4 us (0.952)
  waiting for transfers between devices: 14.7 us -> 12.4 us
    ppermute x3, waiting for transfers between devices: 5.02 us -> 3.67 us  [to_chip(): return lax.ppermute(x, 'ops', other_chip)]
    ppermute x4, starting transfers between devices: 18.1 us -> 17 us  [the longest x2 16.7 us: to_below(): return lax.ppermute(x, BOTH, downward)]
    ppermute x3, starting transfers between devices: 0.72 us -> 1.47 us  [to_chip(): return lax.ppermute(x, 'ops', other_chip)]
    ppermute x2 -> x3, waiting for transfers between devices: 5.1 us -> 4.44 us  [to_core(): return lax.ppermute(x, 'ops', other_core)]
    ppermute x2 -> x3, starting transfers between devices: 3.42 us -> 3.92 us  [to_core(): return lax.ppermute(x, 'ops', other_core)]
    pallas_call x6 -> x11, Pallas kernels: 1.3 us -> 1.33 us  [small_call(): pl.pallas_call(kernel, out_shape=shapes, in_specs=[vmem] * len(args), out...]
  transfers between devices with their start and end apart: 9 -> 10, of which waited for: 5 -> 5; matrix products, arithmetic and copies ran while one was open for 0% -> 0% of each run, Pallas kernels for 1% -> 1%
where the time goes in v3:
time: 45.4 us; the launch traced here: 45.1 us
  starting transfers between devices  22.4 us (49%)
  waiting for transfers between devices  12.4 us (27%)
  Pallas kernels  10.3 us (23%)
    ppermute x2, starting transfers between devices, to_below(): return lax.ppermute(x, BOTH, downward)  16.7 us
    pallas_call x1, Pallas kernels, terms_call(): pl.pallas_call(terms_kernel, out_shape=(shape(3 * sectors, 2), shape(3 *...  8.96 us
    ppermute x3, waiting for transfers between devices, to_core(): return lax.ppermute(x, 'ops', other_core)  4.44 us
    ppermute x2, waiting for transfers between devices, to_above(): return lax.ppermute(x, BOTH, upward)  4.25 us
    ppermute x3, starting transfers between devices, to_core(): return lax.ppermute(x, 'ops', other_core)  3.92 us
    ppermute x3, waiting for transfers between devices, to_chip(): return lax.ppermute(x, 'ops', other_chip)  3.67 us
    ppermute x3, starting transfers between devices, to_chip(): return lax.ppermute(x, 'ops', other_chip)  1.47 us
    pallas_call x11, Pallas kernels, small_call(): pl.pallas_call(kernel, out_shape=shapes, in_specs=[vmem] * len(args), out...  1.33 us
  transfers between devices with their start and end apart: 10, of which 5 were waited for; matrix products, arithmetic and copies ran while one was open for 0% of the time, Pallas kernels for 1%

profile of v3, /device:TPU:1, one launch (start us, length us, event | category | flops | bytes accessed | tf_op | source)
XLA Modules:
  0.0 45.1 jit_solution(12034905752592579700)
XLA Ops:
  0.0 9.0 %terms.1 = (f32[12,2,64,256]{3,2,1,0:T(8,128)S(1)}, f32[12,2,64,256]{3,2,1,0:T(8,128)S(1)}, f32[8,2,64,256]{3,2,1,0:T(8,128)S(1)}, f32[8,2,64,256]{3,2,1,0:T(8,1...) custom-call(s32[1]{0:T(128)} %bitcast.me_ref, s32[2,256]{1,0:T(2,128)} %dims_hbm.1, ...), custom_call_target="tpu_custom_call" | custom-call | flops 5368709120 | bytes 10485760 | tf_op jit(solution)/shard_map/terms/pallas_call | solution.py:124
  9.0 3.3 %collective-permute-start.1 = (f32[8,2,64,256]{3,2,1,0:T(8,128)S(1)}, f32[8,2,64,256]{3,2,1,0:T(8,128)S(1)}, u32[]{:S(2)}, u32[]{:S(2)}) collective-permute-start(f32[8,2,64,256]{3,2,1,0:T(8,128)S(1)} %get-tuple-element.19), channel_id=1, source_target_pairs={{0,64},{64,0},{128,192},{192,128},{1,65},{65,1},{129,193},{193,129... | collective-permute-start | bytes 3145736 | tf_op jit(solution)/shard_map/ppermute | solution.py:242
  12.3 2.3 %collective-permute-done.1.got = f32[8,2,64,256]{3,2,1,0:T(8,128)S(1)} collective-permute-done((f32[8,2,64,256]{3,2,1,0:T(8,128)S(1)}, f32[8,2,64,256]{3,2,1,0:T(8,128)S(1)}, u32[]{:S(2)}, u32[]{:S(2)}) %collective-permute-start.1) | collective-permute-done | bytes 1048608 | tf_op jit(solution)/shard_map/ppermute | solution.py:242
  14.6 0.1 far1.1
  14.6 0.5 %collective-permute-start.2 = (f32[8,2,64,256]{3,2,1,0:T(8,128)S(1)}, f32[8,2,64,256]{3,2,1,0:T(8,128)S(1)}, u32[]{:S(2)}, u32[]{:S(2)}) collective-permute-start(f32[8,2,64,256]{3,2,1,0:T(8,128)S(1)} %get-tuple-element.21), channel_id=1, source_target_pairs={{0,64},{64,0},{128,192},{192,128},{1,65},{65,1},{129,193},{193,129... | collective-permute-start | bytes 3145736 | tf_op jit(solution)/shard_map/ppermute | solution.py:242
  15.1 0.1 collective-permute-start
  15.2 0.0 collective-permute-start.6
  15.2 2.1 %collective-permute-done.2.got = f32[8,2,64,256]{3,2,1,0:T(8,128)S(1)} collective-permute-done((f32[8,2,64,256]{3,2,1,0:T(8,128)S(1)}, f32[8,2,64,256]{3,2,1,0:T(8,128)S(1)}, u32[]{:S(2)}, u32[]{:S(2)}) %collective-permute-start.2) | collective-permute-done | bytes 1048608 | tf_op jit(solution)/shard_map/ppermute | solution.py:242
  17.4 0.1 up0.1
  17.4 0.1 collective-permute-start.3
  17.5 0.1 down0.1
  17.6 8.6 %collective-permute-start.4 = (f32[4,2,64,256]{3,2,1,0:T(8,128)S(1)}, f32[4,2,64,256]{3,2,1,0:T(8,128)S(1)}, u32[]{:S(2)}, u32[]{:S(2)}) collective-permute-start(f32[4,2,64,256]{3,2,1,0:T(8,128)S(1)} %down0.1), channel_id=1, source_target_pairs={{1,0},{2,1},{3,2},{4,3},{5,4},{6,5},{7,6},{136,7},{9,8},{10,9},{11... | collective-permute-start | bytes 1572872 | tf_op jit(solution)/shard_map/ppermute | solution.py:251
  26.2 0.0 collective-permute-done.got
  26.2 2.2 %collective-permute-done.6.far = f32[8,64,256]{2,1,0:T(8,128)S(1)} collective-permute-done((f32[8,64,256]{2,1,0:T(8,128)S(1)}, f32[8,64,256]{2,1,0:T(8,128)S(1)}, u32[]{:S(2)}, u32[]{:S(2)}) %collective-permute-start.6) | collective-permute-done | bytes 524320 | tf_op jit(solution)/shard_map/ppermute | solution.py:245
  28.5 0.3 collective-permute-start.8
  28.7 1.1 %collective-permute-start.7 = (f32[4,64,256]{2,1,0:T(8,128)S(1)}, f32[4,64,256]{2,1,0:T(8,128)S(1)}, u32[]{:S(2)}, u32[]{:S(2)}) collective-permute-start(f32[4,64,256]{2,1,0:T(8,128)S(1)} %own_far1.1), channel_id=1, source_target_pairs={{0,128},{64,192},{128,0},{192,64},{1,129},{65,193},{129,1},{193,65... | collective-permute-start | bytes 786440 | tf_op jit(solution)/shard_map/ppermute | solution.py:245
  29.9 8.1 %collective-permute-start.9 = (f32[4,64,256]{2,1,0:T(8,128)S(1)}, f32[4,64,256]{2,1,0:T(8,128)S(1)}, u32[]{:S(2)}, u32[]{:S(2)}) collective-permute-start(f32[4,64,256]{2,1,0:T(8,128)S(1)} %down1.1), channel_id=1, source_target_pairs={{1,0},{2,1},{3,2},{4,3},{5,4},{6,5},{7,6},{136,7},{9,8},{10,9},{11... | collective-permute-start | bytes 786440 | tf_op jit(solution)/shard_map/ppermute | solution.py:251
  38.0 0.0 collective-permute-done.3.below
  38.0 0.1 base0.1.base
  38.1 0.0 collective-permute-done.4.above.above0
  38.1 0.4 collective-permute-start.5
  38.5 4.2 %collective-permute-done.8.below = f32[4,64,256]{2,1,0:T(8,128)S(1)} collective-permute-done((f32[4,64,256]{2,1,0:T(8,128)S(1)}, f32[4,64,256]{2,1,0:T(8,128)S(1)}, u32[]{:S(2)}, u32[]{:S(2)}) %collective-permute-start.8) | collective-permute-done | bytes 262176 | tf_op jit(solution)/shard_map/ppermute | solution.py:248
  42.7 0.0 collective-permute-done.7.far
  42.8 0.0 collective-permute-done.9.above
  42.8 1.5 %collective-permute-done.5.far0 = f32[4,64,256]{2,1,0:T(8,128)S(1)} collective-permute-done((f32[4,64,256]{2,1,0:T(8,128)S(1)}, f32[4,64,256]{2,1,0:T(8,128)S(1)}, u32[]{:S(2)}, u32[]{:S(2)}) %collective-permute-start.5) | collective-permute-done | bytes 262176 | tf_op jit(solution)/shard_map/ppermute | solution.py:245
  44.3 0.9 %finish.1 = f32[2,4,64,256]{3,2,1,0:T(8,128)} custom-call(f32[4,2,64,256]{3,2,1,0:T(8,128)S(1)} %base0.1.base, f32[4,2,64,256]{3,2,1,0:T(8,128)S(1)} %collective-permute-done.4.above.above0, f32[4,64,256]{2,1,0:T(8,128)S(1)} %collective-permute-done.5.far0, f32[4,64,256]{2,1,0:T(8,128)S(1)} %sum1.1.base1, f32[4,64,256]{2,1,0:T(8,128)S(1)} %get-tuple-element.26.inside), custom_call_target="tpu_custom_call" | custom-call | flops 458752 | bytes 1835008 | tf_op jit(solution)/shard_map/finish/pallas_call | solution.py:159
  (6 shorter events, 0.2 us)
Async XLA Ops:
  9.0 5.6 %collective-permute-start.1 = (f32[8,2,64,256]{3,2,1,0:T(8,128)S(1)}, f32[8,2,64,256]{3,2,1,0:T(8,128)S(1)}, u32[]{:S(2)}, u32[]{:S(2)}) collective-permute-start(f32[8,2,64,256]{3,2,1,0:T(8,128)S(1)} %get-tuple-element.19), channel_id=1, source_target_pairs={{0,64},{64,0},{128,192},{192,128},{1,65},{65,1},{129,193},{193,129... | collective-permute-start | bytes 3145736 | tf_op jit(solution)/shard_map/ppermute | solution.py:242
  14.6 2.7 %collective-permute-start.2 = (f32[8,2,64,256]{3,2,1,0:T(8,128)S(1)}, f32[8,2,64,256]{3,2,1,0:T(8,128)S(1)}, u32[]{:S(2)}, u32[]{:S(2)}) collective-permute-start(f32[8,2,64,256]{3,2,1,0:T(8,128)S(1)} %get-tuple-element.21), channel_id=1, source_target_pairs={{0,64},{64,0},{128,192},{192,128},{1,65},{65,1},{129,193},{193,129... | collective-permute-start | bytes 3145736 | tf_op jit(solution)/shard_map/ppermute | solution.py:242
  15.1 11.1 %collective-permute-start = (f32[2,4,2,64,256]{4,3,2,1,0:T(8,128)S(1)}, f32[2,4,2,64,256]{4,3,2,1,0:T(8,128)S(1)}, u32[]{:S(2)}, u32[]{:S(2)}) collective-permute-start(f32[2,4,2,64,256]{4,3,2,1,0:T(8,128)S(1)} %get-tuple-element.17), channel_id=1, source_target_pairs={{0,64},{64,0},{128,192},{192,128},{1,65},{65,1},{129,193},{193,129... | collective-permute-start | bytes 3145736 | tf_op jit(solution)/shard_map/ppermute | solution.py:242
  15.2 13.1 %collective-permute-start.6 = (f32[8,64,256]{2,1,0:T(8,128)S(1)}, f32[8,64,256]{2,1,0:T(8,128)S(1)}, u32[]{:S(2)}, u32[]{:S(2)}) collective-permute-start(f32[8,64,256]{2,1,0:T(8,128)S(1)} %far1.1), channel_id=1, source_target_pairs={{0,128},{64,192},{128,0},{192,64},{1,129},{65,193},{129,1},{193,65... | collective-permute-start | bytes 1572872 | tf_op jit(solution)/shard_map/ppermute | solution.py:245
  17.4 20.6 %collective-permute-start.3 = (f32[4,2,64,256]{3,2,1,0:T(8,128)S(1)}, f32[4,2,64,256]{3,2,1,0:T(8,128)S(1)}, u32[]{:S(2)}, u32[]{:S(2)}) collective-permute-start(f32[4,2,64,256]{3,2,1,0:T(8,128)S(1)} %up0.1), channel_id=1, source_target_pairs={{0,1},{1,2},{2,3},{3,4},{4,5},{5,6},{6,7},{7,136},{8,9},{9,10},{10... | collective-permute-start | bytes 1572872 | tf_op jit(solution)/shard_map/ppermute | solution.py:248
  17.6 20.5 %collective-permute-start.4 = (f32[4,2,64,256]{3,2,1,0:T(8,128)S(1)}, f32[4,2,64,256]{3,2,1,0:T(8,128)S(1)}, u32[]{:S(2)}, u32[]{:S(2)}) collective-permute-start(f32[4,2,64,256]{3,2,1,0:T(8,128)S(1)} %down0.1), channel_id=1, source_target_pairs={{1,0},{2,1},{3,2},{4,3},{5,4},{6,5},{7,6},{136,7},{9,8},{10,9},{11... | collective-permute-start | bytes 1572872 | tf_op jit(solution)/shard_map/ppermute | solution.py:251
  28.5 14.3 %collective-permute-start.8 = (f32[4,64,256]{2,1,0:T(8,128)S(1)}, f32[4,64,256]{2,1,0:T(8,128)S(1)}, u32[]{:S(2)}, u32[]{:S(2)}) collective-permute-start(f32[4,64,256]{2,1,0:T(8,128)S(1)} %up1.1), channel_id=1, source_target_pairs={{0,1},{1,2},{2,3},{3,4},{4,5},{5,6},{6,7},{7,136},{8,9},{9,10},{10... | collective-permute-start | bytes 786440 | tf_op jit(solution)/shard_map/ppermute | solution.py:248
  28.7 14.0 %collective-permute-start.7 = (f32[4,64,256]{2,1,0:T(8,128)S(1)}, f32[4,64,256]{2,1,0:T(8,128)S(1)}, u32[]{:S(2)}, u32[]{:S(2)}) collective-permute-start(f32[4,64,256]{2,1,0:T(8,128)S(1)} %own_far1.1), channel_id=1, source_target_pairs={{0,128},{64,192},{128,0},{192,64},{1,129},{65,193},{129,1},{193,65... | collective-permute-start | bytes 786440 | tf_op jit(solution)/shard_map/ppermute | solution.py:245
  29.9 12.9 %collective-permute-start.9 = (f32[4,64,256]{2,1,0:T(8,128)S(1)}, f32[4,64,256]{2,1,0:T(8,128)S(1)}, u32[]{:S(2)}, u32[]{:S(2)}) collective-permute-start(f32[4,64,256]{2,1,0:T(8,128)S(1)} %down1.1), channel_id=1, source_target_pairs={{1,0},{2,1},{3,2},{4,3},{5,4},{6,5},{7,6},{136,7},{9,8},{10,9},{11... | collective-permute-start | bytes 786440 | tf_op jit(solution)/shard_map/ppermute | solution.py:251
  38.1 6.2 %collective-permute-start.5 = (f32[4,64,256]{2,1,0:T(8,128)S(1)}, f32[4,64,256]{2,1,0:T(8,128)S(1)}, u32[]{:S(2)}, u32[]{:S(2)}) collective-permute-start(f32[4,64,256]{2,1,0:T(8,128)S(1)} %own_far0.1), channel_id=1, source_target_pairs={{0,128},{64,192},{128,0},{192,64},{1,129},{65,193},{129,1},{193,65... | collective-permute-start | bytes 786440 | tf_op jit(solution)/shard_map/ppermute | solution.py:245

commit v4 on v3

--- a/solution.py
+++ b/solution.py
@@ -15,20 +15,59 @@
 NN = (((1,), (0,)), ((), ()))
 
 
-def terms_kernel(
+def own_place(me_ref, peers, sectors):
+    sec, ops = me_ref[0] % peers, me_ref[0] // peers
+    return ops % 2, ops // 2, sec * sectors, sec % Z_RUN
+
+
+def add_terms(parts, wait, place_of, keep, sums, masked, left_buf, right_buf, half, core, x_lo, z):
+    sectors, terms, pad, _ = left_buf.shape
+    run = pad // 4
+
+    def first_stage(l, t, u):
+        product = lax.dot_general(masked[l], right_buf[l, t], NT, preferred_element_type=jnp.float32)
+        half[u] = product.astype(jnp.bfloat16)
+
+    def second_stage(l, t, u):
+        place = place_of(l, t)
+        flip = ((place < 0) & (z == 0)) | ((place >= sectors) & (z == Z_RUN - 1))
+        near = x_lo ^ flip.astype(jnp.int32)
+        blocks = [2 * near + core, 2 * (1 - near) + core, 2 * near + 1 - core, 2 * (1 - near) + 1 - core]
+        lhs = jnp.concatenate(
+            [left_buf[l, t, pl.ds(pl.multiple_of(b * run, run), run), :] for b in blocks], axis=0
+        )
+        term = lax.dot_general(lhs, half[u], NN, preferred_element_type=jnp.float32)
+        for q in range(2):
+            keep[place + sectors, q] += term[q * run : (q + 1) * run]
+            sums[place + sectors, q] += term[(2 + q) * run : (3 + q) * run]
+
+    for i, (l, t, number) in enumerate(parts):
+        wait(i, l, t)
+        first_stage(l, t, 0)
+        for u in range(number):
+            if u + 1 < number:
+                first_stage(l, t + u + 1, u + 1)
+            second_stage(l, t + u, u)
+
+
+def give_sums(sums, send, send_own):
+    sectors = send_own.shape[0]
+    send[:sectors] = sums[:sectors]
+    send[sectors:] = sums[2 * sectors :]
+    send_own[...] = sums[sectors : 2 * sectors]
+
+
+def terms1_kernel(
     me_ref, dims_hbm, pair_hbm, wave_ref, left_ref, right_ref,
-    keep0, keep1, send0, send1, send_own, inside,
-    wave_buf, masked, left_buf, right_buf, half, sums, dims_ref, pair_ref,
+    keep, send, send_own, inside, left_buf, right_buf, masked0,
+    wave_buf, masked1, half, sums, dims_ref, pair_ref,
     wave_sem, left_sem, right_sem, dims_sem, pair_sem,
 ):
     terms, sectors, pad, _ = left_ref.shape
     run = pad // 4
     peers = dims_ref.shape[1] // sectors
-    me = me_ref[0]
-    sec, ops = me % peers, me // peers
-    core, x_lo = ops % 2, ops // 2
-    first = sec * sectors
-    z = sec % Z_RUN
+    core, x_lo, first, z = own_place(me_ref, peers, sectors)
+    ops = me_ref[0] // peers
 
     pair_copy = pltpu.make_async_copy(pair_hbm, pair_ref, pair_sem)
     dims_copy = pltpu.make_async_copy(dims_hbm, dims_ref, dims_sem)
@@ -58,34 +97,15 @@
         right_copy(i).start(priority=1)
         left_copy(i).start(priority=1)
 
-    for ref in (keep0, keep1, sums):
+    for ref in (keep, sums):
         ref[...] = jnp.zeros_like(ref)
     rows = lax.broadcasted_iota(jnp.int32, (pad, pad), 0)
     cols = lax.broadcasted_iota(jnp.int32, (pad, pad), 1)
 
     def mask(l):
         valid = (rows < dims_ref[0, first + l]) & (cols < dims_ref[1, first + l])
-        for v in range(2):
-            value = jnp.where(valid, wave_buf[v, l].astype(jnp.float32), 0.0)
-            masked[l, v * pad : (v + 1) * pad] = value.astype(jnp.bfloat16)
-
-    def first_stage(l, t, u):
-        product = lax.dot_general(masked[l], right_buf[l, t], NT, preferred_element_type=jnp.float32)
-        half[u] = product.astype(jnp.bfloat16)
-
-    def second_stage(l, t, u):
-        place = pair_ref[l, t] - first
-        flip = ((place < 0) & (z == 0)) | ((place >= sectors) & (z == Z_RUN - 1))
-        near = x_lo ^ flip.astype(jnp.int32)
-        blocks = [2 * near + core, 2 * (1 - near) + core, 2 * near + 1 - core, 2 * (1 - near) + 1 - core]
-        lhs = jnp.concatenate(
-            [left_buf[l, t, pl.ds(pl.multiple_of(b * run, run), run), :] for b in blocks], axis=0
-        )
-        for v, keep in enumerate((keep0, keep1)):
-            term = lax.dot_general(lhs, half[u, v * pad : (v + 1) * pad], NN, preferred_element_type=jnp.float32)
-            for q in range(2):
-                keep[place + sectors, q] += term[q * run : (q + 1) * run]
-                sums[v, place + sectors, q] += term[(2 + q) * run : (3 + q) * run]
+        for v, masked in enumerate((masked0, masked1)):
+            masked[l] = jnp.where(valid, wave_buf[v, l].astype(jnp.float32), 0.0).astype(jnp.bfloat16)
 
     dims_copy.wait()
     own_rows = lax.broadcasted_iota(jnp.int32, (run, pad), 0) + ops * run
@@ -94,48 +114,68 @@
         valid = (own_rows < dims_ref[0, first + l]) & (own_cols < dims_ref[1, first + l])
         inside[l] = jnp.where(valid, 1.0, 0.0)
     pair_copy.wait()
-    for i, (l, t, number) in enumerate(parts):
+
+    def wait(i, l, t):
         if t == 0:
             wave_copy(l).wait()
         right_copy(i).wait()
         left_copy(i).wait()
         if t == 0:
             mask(l)
-        first_stage(l, t, 0)
-        for u in range(number):
-            if u + 1 < number:
-                first_stage(l, t + u + 1, u + 1)
-            second_stage(l, t + u, u)
-    for v, send in enumerate((send0, send1)):
-        send[:sectors] = sums[v, :sectors]
-        send[sectors:] = sums[v, 2 * sectors :]
-    send_own[...] = sums[:, sectors : 2 * sectors]
-
-
-def terms_call(me, dims, pairing, wave, left, right):
+
+    add_terms(
+        parts, wait, lambda l, t: pair_ref[l, t] - first, keep, sums, masked1, left_buf, right_buf, half, core, x_lo, z
+    )
+    give_sums(sums, send, send_own)
+
+
+def terms0_kernel(peers, me_ref, pair_hbm, left_buf, right_buf, masked0, keep, send, send_own, half, sums, pair_ref, pair_sem):
+    sectors, terms, pad, _ = left_buf.shape
+    core, x_lo, first, z = own_place(me_ref, peers, sectors)
+    pair_copy = pltpu.make_async_copy(pair_hbm, pair_ref, pair_sem)
+    pair_copy.start()
+    for ref in (keep, sums):
+        ref[...] = jnp.zeros_like(ref)
+    pair_copy.wait()
+    add_terms(
+        [(l, 0, terms) for l in range(sectors)], lambda i, l, t: None, lambda l, t: pair_ref[l, t] - first,
+        keep, sums, masked0, left_buf, right_buf, half, core, x_lo, z,
+    )
+    give_sums(sums, send, send_own)
+
+
+def terms_calls(me, dims, pairing, wave, left, right):
     terms, sectors, pad, _ = left.shape
     pairs = terms * sectors
+    peers = dims.shape[1] // sectors
+
     def shape(*leading):
         return jax.ShapeDtypeStruct((*leading, pad // 4, pad), jnp.float32)
 
+    def half_shape(*leading):
+        return jax.ShapeDtypeStruct((*leading, pad, pad), jnp.bfloat16)
+
+    sums = (shape(3 * sectors, 2), shape(2 * sectors, 2), shape(sectors, 2))
     in_hbm = pl.BlockSpec(memory_space=pltpu.HBM)
+    in_smem = pl.BlockSpec(memory_space=pltpu.SMEM)
     vmem = pl.BlockSpec(memory_space=pltpu.VMEM)
-    operands = (dims, pairing.T, wave, left, right)
-    return pl.pallas_call(
-        terms_kernel,
+    me = me.reshape(1)
+    operands = [pltpu.with_memory_space_constraint(x, pltpu.HBM) for x in (dims, pairing.T, wave, left, right)]
+    sums_buf = pltpu.VMEM((3 * sectors, 2, pad // 4, pad), jnp.float32)
+    half_buf = pltpu.VMEM((terms, pad, pad), jnp.bfloat16)
+    cost = pl.CostEstimate(flops=pairs * 4 * pad**3, bytes_accessed=pairs * pad * pad * 4, transcendentals=0)
+    keep1, send1, own1, inside, left, right, masked0 = pl.pallas_call(
+        terms1_kernel,
         out_shape=(
-            shape(3 * sectors, 2), shape(3 * sectors, 2), shape(2 * sectors, 2), shape(2 * sectors, 2),
-            shape(2, sectors, 2), shape(sectors),
+            *sums, shape(sectors), half_shape(sectors, terms), half_shape(sectors, terms), half_shape(sectors)
         ),
-        in_specs=[pl.BlockSpec(memory_space=pltpu.SMEM)] + [in_hbm] * 5,
-        out_specs=(vmem,) * 6,
+        in_specs=[in_smem] + [in_hbm] * 5,
+        out_specs=(vmem,) * 7,
         scratch_shapes=[
             pltpu.VMEM(wave.shape, jnp.bfloat16),
-            pltpu.VMEM((sectors, 2 * pad, pad), jnp.bfloat16),
-            pltpu.VMEM((sectors, terms, pad, pad), jnp.bfloat16),
-            pltpu.VMEM((sectors, terms, pad, pad), jnp.bfloat16),
-            pltpu.VMEM((terms, 2 * pad, pad), jnp.bfloat16),
-            pltpu.VMEM((2, 3 * sectors, 2, pad // 4, pad), jnp.float32),
+            pltpu.VMEM((sectors, pad, pad), jnp.bfloat16),
+            half_buf,
+            sums_buf,
             pltpu.SMEM(dims.shape, jnp.int32),
             pltpu.SMEM((sectors, terms), jnp.int32),
             pltpu.SemaphoreType.DMA((sectors,)),
@@ -144,12 +184,21 @@
             pltpu.SemaphoreType.DMA,
             pltpu.SemaphoreType.DMA,
         ],
-        compiler_params=pltpu.CompilerParams(vmem_limit_bytes=32 * 1024 * 1024),
-        cost_estimate=pl.CostEstimate(
-            flops=pairs * 8 * pad**3, bytes_accessed=pairs * pad * pad * 4, transcendentals=0
-        ),
-        name="terms",
-    )(me.reshape(1), *(pltpu.with_memory_space_constraint(x, pltpu.HBM) for x in operands))
+        compiler_params=pltpu.CompilerParams(vmem_limit_bytes=24 * 1024 * 1024),
+        cost_estimate=cost,
+        name="terms1",
+    )(me, *operands)
+    keep0, send0, own0 = pl.pallas_call(
+        functools.partial(terms0_kernel, peers),
+        out_shape=sums,
+        in_specs=[in_smem, in_hbm, vmem, vmem, vmem],
+        out_specs=(vmem,) * 3,
+        scratch_shapes=[half_buf, sums_buf, pltpu.SMEM((sectors, terms), jnp.int32), pltpu.SemaphoreType.DMA],
+        compiler_params=pltpu.CompilerParams(vmem_limit_bytes=24 * 1024 * 1024),
+        cost_estimate=cost,
+        name="terms0",
+    )(me, operands[1], left, right, masked0)
+    return (keep0, send0, own0), (keep1, send1, own1), inside
 
 
 def small_call(kernel, name, out_shapes, *args):
@@ -196,12 +245,12 @@
 
 def own_far1_kernel(keep, got, out):
     sectors = out.shape[0]
-    out[...] = keep[sectors : 2 * sectors, 1] + got[1, :, 1]
+    out[...] = keep[sectors : 2 * sectors, 1] + got[:, 1]
 
 
 def base0_kernel(keep, got, below, out):
     sectors = out.shape[0]
-    out[...] = keep[sectors : 2 * sectors] + got[0] + below[...]
+    out[...] = keep[sectors : 2 * sectors] + got[...] + below[...]
 
 
 def own_far0_kernel(base, above, out):
@@ -210,7 +259,7 @@
 
 def base1_kernel(keep, got, far, below, out):
     sectors = out.shape[0]
-    out[...] = keep[sectors : 2 * sectors, 0] + got[1, :, 0] + far[...] + below[...]
+    out[...] = keep[sectors : 2 * sectors, 0] + got[:, 0] + far[...] + below[...]
 
 
 def sum1_kernel(base, above, out):
@@ -253,29 +302,32 @@
     def after(first, second):
         return lax.optimization_barrier((first, second))
 
-    keep0, keep1, send0, send1, send_own, inside = terms_call(
+    (keep0, send0, send_own0), (keep1, send1, send_own1), inside = terms_calls(
         lax.axis_index(BOTH), sector_dims, pairing, wavefunction, left_blocks, right_blocks
     )
     got1 = to_core(send1)
-    got = to_core(send_own)
 
     far1 = small_call(far_kernel, "far1", ((2 * sectors, run, pad),), keep1, got1)
     far1, send0 = after(far1, send0)
     got0 = to_core(send0)
     far1 = to_chip(far1)
     below0 = to_above(small_call(up_kernel, "up0", (both,), keep0, got0))
-    above0 = to_below(small_call(down_kernel, "down0", (both,), keep0, got0))
+    down0 = small_call(down_kernel, "down0", (both,), keep0, got0)
+    down0, (send_own1, send_own0) = after(down0, (send_own1, send_own0))
+    above0 = to_below(down0)
+    own_got1 = to_core(send_own1)
+    own_got0 = to_core(send_own0)
 
     below1 = to_above(small_call(near_up_kernel, "up1", (near,), keep1, got1, far1))
-    far1_later, got_later = after(far1, got)
+    far1_later, got_later = after(far1, own_got1)
     own_far1 = small_call(own_far1_kernel, "own_far1", (near,), keep1, got_later)
-    base0 = small_call(base0_kernel, "base0", (both,), keep0, got, below0)
+    base0 = small_call(base0_kernel, "base0", (both,), keep0, own_got0, below0)
     far0 = small_call(own_far0_kernel, "own_far0", (near,), base0, above0)
     own_far1, far1_later = after(own_far1, far1)
     above1 = to_below(small_call(near_down_kernel, "down1", (near,), keep1, got1, far1_later))
     own_far1 = to_chip(own_far1)
     far0 = to_chip(far0)
-    base1 = small_call(base1_kernel, "base1", (near,), keep1, got, own_far1, below1)
+    base1 = small_call(base1_kernel, "base1", (near,), keep1, own_got1, own_far1, below1)
     sum1 = small_call(sum1_kernel, "sum1", (near,), base1, above1)
     return small_call(finish_kernel, "finish", ((2, sectors, run, pad),), base0, above0, far0, sum1, inside)
 

time: 45.4 us -> 46.1 us (1.015)
  Pallas kernels: 10.3 us -> 11.8 us
  waiting for transfers between devices: 12.4 us -> 11.7 us
    ppermute x2, waiting for transfers between devices: 4.25 us -> 6.87 us  [to_above(): return lax.ppermute(x, BOTH, upward)]
    ppermute x3 -> x4, waiting for transfers between devices: 4.44 us -> 2.55 us  [to_core(): return lax.ppermute(x, 'ops', other_core)]
    pallas_call x1 -> x2, Pallas kernels: 8.96 us -> 10.5 us  [the longest x1 6.17 us: terms_calls(): pl.pallas_call(terms1_kernel, out_shape=(*sums, shape(sectors), half_shap...]
    ppermute x3, waiting for transfers between devices: 3.67 us -> 2.26 us  [to_chip(): return lax.ppermute(x, 'ops', other_chip)]
    ppermute x3 -> x4, starting transfers between devices: 3.92 us -> 4.03 us  [to_core(): return lax.ppermute(x, 'ops', other_core)]
  transfers between devices with their start and end apart: 10 -> 11, of which waited for: 5 -> 5; matrix products, arithmetic and copies ran while one was open for 0% -> 0% of each run, Pallas kernels for 1% -> 10%
where the time goes in v4:
time: 46.1 us; the launch traced here: 46 us
  starting transfers between devices  22.3 us (48%)
  Pallas kernels  11.8 us (26%)
  waiting for transfers between devices  11.7 us (25%)
    ppermute x2, starting transfers between devices, to_below(): return lax.ppermute(x, BOTH, downward)  16.8 us
    ppermute x2, waiting for transfers between devices, to_above(): return lax.ppermute(x, BOTH, upward)  6.87 us
    pallas_call x1, Pallas kernels, terms_calls(): pl.pallas_call(terms1_kernel, out_shape=(*sums, shape(sectors), half_shap...  6.17 us
    pallas_call x1, Pallas kernels, terms_calls(): pl.pallas_call(functools.partial(terms0_kernel, peers), out_shape=sums, i...  4.35 us
    ppermute x4, starting transfers between devices, to_core(): return lax.ppermute(x, 'ops', other_core)  4.03 us
    ppermute x4, waiting for transfers between devices, to_core(): return lax.ppermute(x, 'ops', other_core)  2.55 us
    ppermute x3, waiting for transfers between devices, to_chip(): return lax.ppermute(x, 'ops', other_chip)  2.26 us
    ppermute x3, starting transfers between devices, to_chip(): return lax.ppermute(x, 'ops', other_chip)  1.34 us
  transfers between devices with their start and end apart: 11, of which 5 were waited for; matrix products, arithmetic and copies ran while one was open for 0% of the time, Pallas kernels for 10%

profile of v4, /device:TPU:1, one launch (start us, length us, event | category | flops | bytes accessed | tf_op | source)
XLA Modules:
  0.0 46.0 jit_solution(16873120867284646946)
XLA Ops:
  0.0 6.2 %terms1.1 = (f32[12,2,64,256]{3,2,1,0:T(8,128)S(1)}, f32[8,2,64,256]{3,2,1,0:T(8,128)S(1)}, f32[4,2,64,256]{3,2,1,0:T(8,128)S(1)}, f32[4,64,256]{2,1,0:T(8,128)S...) custom-call(s32[1]{0:T(128)} %bitcast.me_ref, ...), custom_call_target="tpu_custom_call" | custom-call | flops 2684354560 | bytes 10485760 | tf_op jit(solution)/shard_map/terms1/pallas_call | solution.py:167
  6.2 3.3 %collective-permute-start = (f32[8,2,64,256]{3,2,1,0:T(8,128)S(1)}, f32[8,2,64,256]{3,2,1,0:T(8,128)S(1)}, u32[]{:S(2)}, u32[]{:S(2)}) collective-permute-start(f32[8,2,64,256]{3,2,1,0:T(8,128)S(1)} %get-tuple-element.28), channel_id=1, source_target_pairs={{0,64},{64,0},{128,192},{192,128},{1,65},{65,1},{129,193},{193,129... | collective-permute-start | bytes 3145736 | tf_op jit(solution)/shard_map/ppermute | solution.py:291
  9.5 4.3 %terms0.1 = (f32[12,2,64,256]{3,2,1,0:T(8,128)S(1)}, f32[8,2,64,256]{3,2,1,0:T(8,128)S(1)}, f32[4,2,64,256]{3,2,1,0:T(8,128)S(1)}) custom-call(s32[1]{0:T(128)} %bitcast.me_ref, s32[4,10]{1,0:T(4,128)} %bitcast.3, bf16[4,10,256,256]{3,2,1,0:T(8,128)(2,1)S(1)} %get-tuple-element.23.left_buf, bf16[4,10,256,256]{3,2,1,0:T(8,128)(2,1)S(1)} %get-tuple-element.24.right_buf, ...), custom_call_target="tpu_custom_call" | custom-call | flops 2684354560 | bytes 10485760 | tf_op jit(solution)/shard_map/terms0/pallas_call | solution.py:191
  13.9 0.0 collective-permute-done.got
  13.9 0.1 far1.1
  13.9 0.1 collective-permute-start.1
  14.0 0.1 collective-permute-start.7
  14.1 2.5 %collective-permute-done.1.got = f32[8,2,64,256]{3,2,1,0:T(8,128)S(1)} collective-permute-done((f32[8,2,64,256]{3,2,1,0:T(8,128)S(1)}, f32[8,2,64,256]{3,2,1,0:T(8,128)S(1)}, u32[]{:S(2)}, u32[]{:S(2)}) %collective-permute-start.1) | collective-permute-done | bytes 1048608 | tf_op jit(solution)/shard_map/ppermute | solution.py:291
  16.7 0.1 down0.1
  16.7 0.2 collective-permute-start.6
  17.0 0.4 collective-permute-start.2
  17.3 0.1 up0.1
  17.4 0.1 collective-permute-start.3
  17.5 8.7 %collective-permute-start.4 = (f32[4,2,64,256]{3,2,1,0:T(8,128)S(1)}, f32[4,2,64,256]{3,2,1,0:T(8,128)S(1)}, u32[]{:S(2)}, u32[]{:S(2)}) collective-permute-start(f32[4,2,64,256]{3,2,1,0:T(8,128)S(1)} %down0.1), channel_id=1, source_target_pairs={{1,0},{2,1},{3,2},{4,3},{5,4},{6,5},{7,6},{136,7},{9,8},{10,9},{11... | collective-permute-start | bytes 1572872 | tf_op jit(solution)/shard_map/ppermute | solution.py:300
  26.2 1.0 %collective-permute-done.7.far = f32[8,64,256]{2,1,0:T(8,128)S(1)} collective-permute-done((f32[8,64,256]{2,1,0:T(8,128)S(1)}, f32[8,64,256]{2,1,0:T(8,128)S(1)}, u32[]{:S(2)}, u32[]{:S(2)}) %collective-permute-start.7) | collective-permute-done | bytes 524320 | tf_op jit(solution)/shard_map/ppermute | solution.py:294
  27.3 0.1 collective-permute-start.9
  27.4 0.0 collective-permute-done.6.got
  27.4 1.2 %collective-permute-start.8 = (f32[4,64,256]{2,1,0:T(8,128)S(1)}, f32[4,64,256]{2,1,0:T(8,128)S(1)}, u32[]{:S(2)}, u32[]{:S(2)}) collective-permute-start(f32[4,64,256]{2,1,0:T(8,128)S(1)} %own_far1.1), channel_id=1, source_target_pairs={{0,128},{64,192},{128,0},{192,64},{1,129},{65,193},{129,1},{193,65... | collective-permute-start | bytes 786440 | tf_op jit(solution)/shard_map/ppermute | solution.py:294
  28.6 0.0 collective-permute-done.2.got
  28.6 8.0 %collective-permute-start.10 = (f32[4,64,256]{2,1,0:T(8,128)S(1)}, f32[4,64,256]{2,1,0:T(8,128)S(1)}, u32[]{:S(2)}, u32[]{:S(2)}) collective-permute-start(f32[4,64,256]{2,1,0:T(8,128)S(1)} %down1.1), channel_id=1, source_target_pairs={{1,0},{2,1},{3,2},{4,3},{5,4},{6,5},{7,6},{136,7},{9,8},{10,9},{11... | collective-permute-start | bytes 786440 | tf_op jit(solution)/shard_map/ppermute | solution.py:300
  36.6 1.5 %collective-permute-done.3.below = f32[4,2,64,256]{3,2,1,0:T(8,128)S(1)} collective-permute-done((f32[4,2,64,256]{3,2,1,0:T(8,128)S(1)}, f32[4,2,64,256]{3,2,1,0:T(8,128)S(1)}, u32[]{:S(2)}, u32[]{:S(2)}) %collective-permute-start.3) | collective-permute-done | bytes 524320 | tf_op jit(solution)/shard_map/ppermute | solution.py:297
  38.1 0.1 base0.1.base
  38.2 0.0 collective-permute-done.4.above.above0
  38.3 0.1 collective-permute-start.5
  38.4 5.4 %collective-permute-done.9.below = f32[4,64,256]{2,1,0:T(8,128)S(1)} collective-permute-done((f32[4,64,256]{2,1,0:T(8,128)S(1)}, f32[4,64,256]{2,1,0:T(8,128)S(1)}, u32[]{:S(2)}, u32[]{:S(2)}) %collective-permute-start.9) | collective-permute-done | bytes 262176 | tf_op jit(solution)/shard_map/ppermute | solution.py:297
  43.7 0.0 collective-permute-done.8.far
  43.8 0.0 collective-permute-done.10.above
  43.8 1.3 %collective-permute-done.5.far0 = f32[4,64,256]{2,1,0:T(8,128)S(1)} collective-permute-done((f32[4,64,256]{2,1,0:T(8,128)S(1)}, f32[4,64,256]{2,1,0:T(8,128)S(1)}, u32[]{:S(2)}, u32[]{:S(2)}) %collective-permute-start.5) | collective-permute-done | bytes 262176 | tf_op jit(solution)/shard_map/ppermute | solution.py:294
  45.1 0.9 %finish.1 = f32[2,4,64,256]{3,2,1,0:T(8,128)} custom-call(f32[4,2,64,256]{3,2,1,0:T(8,128)S(1)} %base0.1.base, f32[4,2,64,256]{3,2,1,0:T(8,128)S(1)} %collective-permute-done.4.above.above0, f32[4,64,256]{2,1,0:T(8,128)S(1)} %collective-permute-done.5.far0, f32[4,64,256]{2,1,0:T(8,128)S(1)} %sum1.1.base1, f32[4,64,256]{2,1,0:T(8,128)S(1)} %get-tuple-element.40.inside), custom_call_target="tpu_custom_call" | custom-call | flops 458752 | bytes 1835008 | tf_op jit(solution)/shard_map/finish/pallas_call | solution.py:208
  (6 shorter events, 0.2 us)
Async XLA Ops:
  6.2 7.7 %collective-permute-start = (f32[8,2,64,256]{3,2,1,0:T(8,128)S(1)}, f32[8,2,64,256]{3,2,1,0:T(8,128)S(1)}, u32[]{:S(2)}, u32[]{:S(2)}) collective-permute-start(f32[8,2,64,256]{3,2,1,0:T(8,128)S(1)} %get-tuple-element.28), channel_id=1, source_target_pairs={{0,64},{64,0},{128,192},{192,128},{1,65},{65,1},{129,193},{193,129... | collective-permute-start | bytes 3145736 | tf_op jit(solution)/shard_map/ppermute | solution.py:291
  13.9 2.7 %collective-permute-start.1 = (f32[8,2,64,256]{3,2,1,0:T(8,128)S(1)}, f32[8,2,64,256]{3,2,1,0:T(8,128)S(1)}, u32[]{:S(2)}, u32[]{:S(2)}) collective-permute-start(f32[8,2,64,256]{3,2,1,0:T(8,128)S(1)} %get-tuple-element.30), channel_id=1, source_target_pairs={{0,64},{64,0},{128,192},{192,128},{1,65},{65,1},{129,193},{193,129... | collective-permute-start | bytes 3145736 | tf_op jit(solution)/shard_map/ppermute | solution.py:291
  14.0 13.2 %collective-permute-start.7 = (f32[8,64,256]{2,1,0:T(8,128)S(1)}, f32[8,64,256]{2,1,0:T(8,128)S(1)}, u32[]{:S(2)}, u32[]{:S(2)}) collective-permute-start(f32[8,64,256]{2,1,0:T(8,128)S(1)} %far1.1), channel_id=1, source_target_pairs={{0,128},{64,192},{128,0},{192,64},{1,129},{65,193},{129,1},{193,65... | collective-permute-start | bytes 1572872 | tf_op jit(solution)/shard_map/ppermute | solution.py:294
  16.7 10.6 %collective-permute-start.6 = (f32[4,2,64,256]{3,2,1,0:T(8,128)S(1)}, f32[4,2,64,256]{3,2,1,0:T(8,128)S(1)}, u32[]{:S(2)}, u32[]{:S(2)}) collective-permute-start(f32[4,2,64,256]{3,2,1,0:T(8,128)S(1)} %get-tuple-element.35), channel_id=1, source_target_pairs={{0,64},{64,0},{128,192},{192,128},{1,65},{65,1},{129,193},{193,129... | collective-permute-start | bytes 1572872 | tf_op jit(solution)/shard_map/ppermute | solution.py:291
  17.0 11.6 %collective-permute-start.2 = (f32[4,2,64,256]{3,2,1,0:T(8,128)S(1)}, f32[4,2,64,256]{3,2,1,0:T(8,128)S(1)}, u32[]{:S(2)}, u32[]{:S(2)}) collective-permute-start(f32[4,2,64,256]{3,2,1,0:T(8,128)S(1)} %get-tuple-element.33), channel_id=1, source_target_pairs={{0,64},{64,0},{128,192},{192,128},{1,65},{65,1},{129,193},{193,129... | collective-permute-start | bytes 1572872 | tf_op jit(solution)/shard_map/ppermute | solution.py:291
  17.4 20.7 %collective-permute-start.3 = (f32[4,2,64,256]{3,2,1,0:T(8,128)S(1)}, f32[4,2,64,256]{3,2,1,0:T(8,128)S(1)}, u32[]{:S(2)}, u32[]{:S(2)}) collective-permute-start(f32[4,2,64,256]{3,2,1,0:T(8,128)S(1)} %up0.1), channel_id=1, source_target_pairs={{0,1},{1,2},{2,3},{3,4},{4,5},{5,6},{6,7},{7,136},{8,9},{9,10},{10... | collective-permute-start | bytes 1572872 | tf_op jit(solution)/shard_map/ppermute | solution.py:297
  17.5 20.7 %collective-permute-start.4 = (f32[4,2,64,256]{3,2,1,0:T(8,128)S(1)}, f32[4,2,64,256]{3,2,1,0:T(8,128)S(1)}, u32[]{:S(2)}, u32[]{:S(2)}) collective-permute-start(f32[4,2,64,256]{3,2,1,0:T(8,128)S(1)} %down0.1), channel_id=1, source_target_pairs={{1,0},{2,1},{3,2},{4,3},{5,4},{6,5},{7,6},{136,7},{9,8},{10,9},{11... | collective-permute-start | bytes 1572872 | tf_op jit(solution)/shard_map/ppermute | solution.py:300
  27.3 16.5 %collective-permute-start.9 = (f32[4,64,256]{2,1,0:T(8,128)S(1)}, f32[4,64,256]{2,1,0:T(8,128)S(1)}, u32[]{:S(2)}, u32[]{:S(2)}) collective-permute-start(f32[4,64,256]{2,1,0:T(8,128)S(1)} %up1.1), channel_id=1, source_target_pairs={{0,1},{1,2},{2,3},{3,4},{4,5},{5,6},{6,7},{7,136},{8,9},{9,10},{10... | collective-permute-start | bytes 786440 | tf_op jit(solution)/shard_map/ppermute | solution.py:297
  27.4 16.3 %collective-permute-start.8 = (f32[4,64,256]{2,1,0:T(8,128)S(1)}, f32[4,64,256]{2,1,0:T(8,128)S(1)}, u32[]{:S(2)}, u32[]{:S(2)}) collective-permute-start(f32[4,64,256]{2,1,0:T(8,128)S(1)} %own_far1.1), channel_id=1, source_target_pairs={{0,128},{64,192},{128,0},{192,64},{1,129},{65,193},{129,1},{193,65... | collective-permute-start | bytes 786440 | tf_op jit(solution)/shard_map/ppermute | solution.py:294
  28.6 15.2 %collective-permute-start.10 = (f32[4,64,256]{2,1,0:T(8,128)S(1)}, f32[4,64,256]{2,1,0:T(8,128)S(1)}, u32[]{:S(2)}, u32[]{:S(2)}) collective-permute-start(f32[4,64,256]{2,1,0:T(8,128)S(1)} %down1.1), channel_id=1, source_target_pairs={{1,0},{2,1},{3,2},{4,3},{5,4},{6,5},{7,6},{136,7},{9,8},{10,9},{11... | collective-permute-start | bytes 786440 | tf_op jit(solution)/shard_map/ppermute | solution.py:300
  38.3 6.9 %collective-permute-start.5 = (f32[4,64,256]{2,1,0:T(8,128)S(1)}, f32[4,64,256]{2,1,0:T(8,128)S(1)}, u32[]{:S(2)}, u32[]{:S(2)}) collective-permute-start(f32[4,64,256]{2,1,0:T(8,128)S(1)} %own_far0.1), channel_id=1, source_target_pairs={{0,128},{64,192},{128,0},{192,64},{1,129},{65,193},{129,1},{193,65... | collective-permute-start | bytes 786440 | tf_op jit(solution)/shard_map/ppermute | solution.py:294

commit v5 on v4

--- a/solution.py
+++ b/solution.py
@@ -306,17 +306,16 @@
         lax.axis_index(BOTH), sector_dims, pairing, wavefunction, left_blocks, right_blocks
     )
     got1 = to_core(send1)
-
+    own_got1 = to_core(send_own1)
+    own_got0 = to_core(send_own0)
+
+    got1, own_got1 = after(got1, own_got1)
     far1 = small_call(far_kernel, "far1", ((2 * sectors, run, pad),), keep1, got1)
     far1, send0 = after(far1, send0)
     got0 = to_core(send0)
     far1 = to_chip(far1)
     below0 = to_above(small_call(up_kernel, "up0", (both,), keep0, got0))
-    down0 = small_call(down_kernel, "down0", (both,), keep0, got0)
-    down0, (send_own1, send_own0) = after(down0, (send_own1, send_own0))
-    above0 = to_below(down0)
-    own_got1 = to_core(send_own1)
-    own_got0 = to_core(send_own0)
+    above0 = to_below(small_call(down_kernel, "down0", (both,), keep0, got0))
 
     below1 = to_above(small_call(near_up_kernel, "up1", (near,), keep1, got1, far1))
     far1_later, got_later = after(far1, own_got1)

time: 46.1 us -> 45 us (0.976)
  waiting for transfers between devices: 11.7 us -> 10.3 us
    ppermute x2, waiting for transfers between devices: 6.87 us -> 4.52 us  [to_above(): return lax.ppermute(x, BOTH, upward)]
    ppermute x3, waiting for transfers between devices: 2.26 us -> 3.68 us  [to_chip(): return lax.ppermute(x, 'ops', other_chip)]
  transfers between devices with their start and end apart: 11 -> 11, of which waited for: 5 -> 4; matrix products, arithmetic and copies ran while one was open for 0% -> 0% of each run, Pallas kernels for 10% -> 11%
where the time goes in v5:
time: 45 us; the launch traced here: 44.9 us
  starting transfers between devices  22.6 us (50%)
  Pallas kernels  11.8 us (26%)
  waiting for transfers between devices  10.3 us (23%)
    ppermute x2, starting transfers between devices, to_below(): return lax.ppermute(x, BOTH, downward)  16.8 us
    pallas_call x1, Pallas kernels, terms_calls(): pl.pallas_call(terms1_kernel, out_shape=(*sums, shape(sectors), half_shap...  6.17 us
    ppermute x2, waiting for transfers between devices, to_above(): return lax.ppermute(x, BOTH, upward)  4.52 us
    pallas_call x1, Pallas kernels, terms_calls(): pl.pallas_call(functools.partial(terms0_kernel, peers), out_shape=sums, i...  4.35 us
    ppermute x4, starting transfers between devices, to_core(): return lax.ppermute(x, 'ops', other_core)  4.13 us
    ppermute x3, waiting for transfers between devices, to_chip(): return lax.ppermute(x, 'ops', other_chip)  3.68 us
    ppermute x4, waiting for transfers between devices, to_core(): return lax.ppermute(x, 'ops', other_core)  2.09 us
    ppermute x3, starting transfers between devices, to_chip(): return lax.ppermute(x, 'ops', other_chip)  1.49 us
  transfers between devices with their start and end apart: 11, of which 4 were waited for; matrix products, arithmetic and copies ran while one was open for 0% of the time, Pallas kernels for 11%

profile of v5, /device:TPU:1, one launch (start us, length us, event | category | flops | bytes accessed | tf_op | source)
XLA Modules:
  0.0 44.9 jit_solution(7627934593307857701)
XLA Ops:
  0.0 6.2 %terms1.1 = (f32[12,2,64,256]{3,2,1,0:T(8,128)S(1)}, f32[8,2,64,256]{3,2,1,0:T(8,128)S(1)}, f32[4,2,64,256]{3,2,1,0:T(8,128)S(1)}, f32[4,64,256]{2,1,0:T(8,128)S...) custom-call(s32[1]{0:T(128)} %bitcast.me_ref, ...), custom_call_target="tpu_custom_call" | custom-call | flops 2684354560 | bytes 10485760 | tf_op jit(solution)/shard_map/terms1/pallas_call | solution.py:167
  6.2 3.3 %collective-permute-start.1 = (f32[8,2,64,256]{3,2,1,0:T(8,128)S(1)}, f32[8,2,64,256]{3,2,1,0:T(8,128)S(1)}, u32[]{:S(2)}, u32[]{:S(2)}) collective-permute-start(f32[8,2,64,256]{3,2,1,0:T(8,128)S(1)} %get-tuple-element.28), channel_id=1, source_target_pairs={{0,64},{64,0},{128,192},{192,128},{1,65},{65,1},{129,193},{193,129... | collective-permute-start | bytes 3145736 | tf_op jit(solution)/shard_map/ppermute | solution.py:291
  9.5 0.1 collective-permute-start.2
  9.6 4.3 %terms0.1 = (f32[12,2,64,256]{3,2,1,0:T(8,128)S(1)}, f32[8,2,64,256]{3,2,1,0:T(8,128)S(1)}, f32[4,2,64,256]{3,2,1,0:T(8,128)S(1)}) custom-call(s32[1]{0:T(128)} %bitcast.me_ref, s32[4,10]{1,0:T(4,128)} %bitcast.3, bf16[4,10,256,256]{3,2,1,0:T(8,128)(2,1)S(1)} %get-tuple-element.22.left_buf, bf16[4,10,256,256]{3,2,1,0:T(8,128)(2,1)S(1)} %get-tuple-element.23.right_buf, ...), custom_call_target="tpu_custom_call" | custom-call | flops 2684354560 | bytes 10485760 | tf_op jit(solution)/shard_map/terms0/pallas_call | solution.py:191
  14.0 0.0 collective-permute-done.2.got
  14.0 0.0 collective-permute-done.1.got
  14.0 0.1 far1.1
  14.0 0.5 %collective-permute-start.3 = (f32[8,2,64,256]{3,2,1,0:T(8,128)S(1)}, f32[8,2,64,256]{3,2,1,0:T(8,128)S(1)}, u32[]{:S(2)}, u32[]{:S(2)}) collective-permute-start(f32[8,2,64,256]{3,2,1,0:T(8,128)S(1)} %get-tuple-element.32), channel_id=1, source_target_pairs={{0,64},{64,0},{128,192},{192,128},{1,65},{65,1},{129,193},{193,129... | collective-permute-start | bytes 3145736 | tf_op jit(solution)/shard_map/ppermute | solution.py:291
  14.5 0.0 collective-permute-start.7
  14.5 0.2 collective-permute-start
  14.7 2.1 %collective-permute-done.3.got = f32[8,2,64,256]{3,2,1,0:T(8,128)S(1)} collective-permute-done((f32[8,2,64,256]{3,2,1,0:T(8,128)S(1)}, f32[8,2,64,256]{3,2,1,0:T(8,128)S(1)}, u32[]{:S(2)}, u32[]{:S(2)}) %collective-permute-start.3) | collective-permute-done | bytes 1048608 | tf_op jit(solution)/shard_map/ppermute | solution.py:291
  16.8 0.1 up0.1
  16.9 0.1 collective-permute-start.4
  17.0 0.1 down0.1
  17.0 8.7 %collective-permute-start.5 = (f32[4,2,64,256]{3,2,1,0:T(8,128)S(1)}, f32[4,2,64,256]{3,2,1,0:T(8,128)S(1)}, u32[]{:S(2)}, u32[]{:S(2)}) collective-permute-start(f32[4,2,64,256]{3,2,1,0:T(8,128)S(1)} %down0.1), channel_id=1, source_target_pairs={{1,0},{2,1},{3,2},{4,3},{5,4},{6,5},{7,6},{136,7},{9,8},{10,9},{11... | collective-permute-start | bytes 1572872 | tf_op jit(solution)/shard_map/ppermute | solution.py:300
  25.8 2.2 %collective-permute-done.7.far = f32[8,64,256]{2,1,0:T(8,128)S(1)} collective-permute-done((f32[8,64,256]{2,1,0:T(8,128)S(1)}, f32[8,64,256]{2,1,0:T(8,128)S(1)}, u32[]{:S(2)}, u32[]{:S(2)}) %collective-permute-start.7) | collective-permute-done | bytes 524320 | tf_op jit(solution)/shard_map/ppermute | solution.py:294
  28.1 0.1 collective-permute-start.9
  28.2 1.1 %collective-permute-start.8 = (f32[4,64,256]{2,1,0:T(8,128)S(1)}, f32[4,64,256]{2,1,0:T(8,128)S(1)}, u32[]{:S(2)}, u32[]{:S(2)}) collective-permute-start(f32[4,64,256]{2,1,0:T(8,128)S(1)} %own_far1.1), channel_id=1, source_target_pairs={{0,128},{64,192},{128,0},{192,64},{1,129},{65,193},{129,1},{193,65... | collective-permute-start | bytes 786440 | tf_op jit(solution)/shard_map/ppermute | solution.py:294
  29.3 0.0 collective-permute-done.got
  29.3 8.1 %collective-permute-start.10 = (f32[4,64,256]{2,1,0:T(8,128)S(1)}, f32[4,64,256]{2,1,0:T(8,128)S(1)}, u32[]{:S(2)}, u32[]{:S(2)}) collective-permute-start(f32[4,64,256]{2,1,0:T(8,128)S(1)} %down1.1), channel_id=1, source_target_pairs={{1,0},{2,1},{3,2},{4,3},{5,4},{6,5},{7,6},{136,7},{9,8},{10,9},{11... | collective-permute-start | bytes 786440 | tf_op jit(solution)/shard_map/ppermute | solution.py:300
  37.4 0.0 collective-permute-done.4.below
  37.4 0.1 base0.1.base
  37.5 0.0 collective-permute-done.5.above.above0
  37.6 0.4 collective-permute-start.6
  38.0 4.5 %collective-permute-done.9.below = f32[4,64,256]{2,1,0:T(8,128)S(1)} collective-permute-done((f32[4,64,256]{2,1,0:T(8,128)S(1)}, f32[4,64,256]{2,1,0:T(8,128)S(1)}, u32[]{:S(2)}, u32[]{:S(2)}) %collective-permute-start.9) | collective-permute-done | bytes 262176 | tf_op jit(solution)/shard_map/ppermute | solution.py:297
  42.5 0.0 collective-permute-done.8.far
  42.6 0.0 collective-permute-done.10.above
  42.6 1.4 %collective-permute-done.6.far0 = f32[4,64,256]{2,1,0:T(8,128)S(1)} collective-permute-done((f32[4,64,256]{2,1,0:T(8,128)S(1)}, f32[4,64,256]{2,1,0:T(8,128)S(1)}, u32[]{:S(2)}, u32[]{:S(2)}) %collective-permute-start.6) | collective-permute-done | bytes 262176 | tf_op jit(solution)/shard_map/ppermute | solution.py:294
  44.0 0.9 %finish.1 = f32[2,4,64,256]{3,2,1,0:T(8,128)} custom-call(f32[4,2,64,256]{3,2,1,0:T(8,128)S(1)} %base0.1.base, f32[4,2,64,256]{3,2,1,0:T(8,128)S(1)} %collective-permute-done.5.above.above0, f32[4,64,256]{2,1,0:T(8,128)S(1)} %collective-permute-done.6.far0, f32[4,64,256]{2,1,0:T(8,128)S(1)} %sum1.1.base1, f32[4,64,256]{2,1,0:T(8,128)S(1)} %get-tuple-element.38.inside), custom_call_target="tpu_custom_call" | custom-call | flops 458752 | bytes 1835008 | tf_op jit(solution)/shard_map/finish/pallas_call | solution.py:208
  (6 shorter events, 0.2 us)
Async XLA Ops:
  6.2 7.8 %collective-permute-start.1 = (f32[8,2,64,256]{3,2,1,0:T(8,128)S(1)}, f32[8,2,64,256]{3,2,1,0:T(8,128)S(1)}, u32[]{:S(2)}, u32[]{:S(2)}) collective-permute-start(f32[8,2,64,256]{3,2,1,0:T(8,128)S(1)} %get-tuple-element.28), channel_id=1, source_target_pairs={{0,64},{64,0},{128,192},{192,128},{1,65},{65,1},{129,193},{193,129... | collective-permute-start | bytes 3145736 | tf_op jit(solution)/shard_map/ppermute | solution.py:291
  9.5 4.5 %collective-permute-start.2 = (f32[4,2,64,256]{3,2,1,0:T(8,128)S(1)}, f32[4,2,64,256]{3,2,1,0:T(8,128)S(1)}, u32[]{:S(2)}, u32[]{:S(2)}) collective-permute-start(f32[4,2,64,256]{3,2,1,0:T(8,128)S(1)} %get-tuple-element.29), channel_id=1, source_target_pairs={{0,64},{64,0},{128,192},{192,128},{1,65},{65,1},{129,193},{193,129... | collective-permute-start | bytes 1572872 | tf_op jit(solution)/shard_map/ppermute | solution.py:291
  14.0 2.8 %collective-permute-start.3 = (f32[8,2,64,256]{3,2,1,0:T(8,128)S(1)}, f32[8,2,64,256]{3,2,1,0:T(8,128)S(1)}, u32[]{:S(2)}, u32[]{:S(2)}) collective-permute-start(f32[8,2,64,256]{3,2,1,0:T(8,128)S(1)} %get-tuple-element.32), channel_id=1, source_target_pairs={{0,64},{64,0},{128,192},{192,128},{1,65},{65,1},{129,193},{193,129... | collective-permute-start | bytes 3145736 | tf_op jit(solution)/shard_map/ppermute | solution.py:291
  14.5 13.5 %collective-permute-start.7 = (f32[8,64,256]{2,1,0:T(8,128)S(1)}, f32[8,64,256]{2,1,0:T(8,128)S(1)}, u32[]{:S(2)}, u32[]{:S(2)}) collective-permute-start(f32[8,64,256]{2,1,0:T(8,128)S(1)} %far1.1), channel_id=1, source_target_pairs={{0,128},{64,192},{128,0},{192,64},{1,129},{65,193},{129,1},{193,65... | collective-permute-start | bytes 1572872 | tf_op jit(solution)/shard_map/ppermute | solution.py:294
  14.5 14.8 %collective-permute-start = (f32[4,2,64,256]{3,2,1,0:T(8,128)S(1)}, f32[4,2,64,256]{3,2,1,0:T(8,128)S(1)}, u32[]{:S(2)}, u32[]{:S(2)}) collective-permute-start(f32[4,2,64,256]{3,2,1,0:T(8,128)S(1)} %get-tuple-element.26), channel_id=1, source_target_pairs={{0,64},{64,0},{128,192},{192,128},{1,65},{65,1},{129,193},{193,129... | collective-permute-start | bytes 1572872 | tf_op jit(solution)/shard_map/ppermute | solution.py:291
  16.9 20.6 %collective-permute-start.4 = (f32[4,2,64,256]{3,2,1,0:T(8,128)S(1)}, f32[4,2,64,256]{3,2,1,0:T(8,128)S(1)}, u32[]{:S(2)}, u32[]{:S(2)}) collective-permute-start(f32[4,2,64,256]{3,2,1,0:T(8,128)S(1)} %up0.1), channel_id=1, source_target_pairs={{0,1},{1,2},{2,3},{3,4},{4,5},{5,6},{6,7},{7,136},{8,9},{9,10},{10... | collective-permute-start | bytes 1572872 | tf_op jit(solution)/shard_map/ppermute | solution.py:297
  17.0 20.5 %collective-permute-start.5 = (f32[4,2,64,256]{3,2,1,0:T(8,128)S(1)}, f32[4,2,64,256]{3,2,1,0:T(8,128)S(1)}, u32[]{:S(2)}, u32[]{:S(2)}) collective-permute-start(f32[4,2,64,256]{3,2,1,0:T(8,128)S(1)} %down0.1), channel_id=1, source_target_pairs={{1,0},{2,1},{3,2},{4,3},{5,4},{6,5},{7,6},{136,7},{9,8},{10,9},{11... | collective-permute-start | bytes 1572872 | tf_op jit(solution)/shard_map/ppermute | solution.py:300
  28.1 14.4 %collective-permute-start.9 = (f32[4,64,256]{2,1,0:T(8,128)S(1)}, f32[4,64,256]{2,1,0:T(8,128)S(1)}, u32[]{:S(2)}, u32[]{:S(2)}) collective-permute-start(f32[4,64,256]{2,1,0:T(8,128)S(1)} %up1.1), channel_id=1, source_target_pairs={{0,1},{1,2},{2,3},{3,4},{4,5},{5,6},{6,7},{7,136},{8,9},{9,10},{10... | collective-permute-start | bytes 786440 | tf_op jit(solution)/shard_map/ppermute | solution.py:297
  28.2 14.3 %collective-permute-start.8 = (f32[4,64,256]{2,1,0:T(8,128)S(1)}, f32[4,64,256]{2,1,0:T(8,128)S(1)}, u32[]{:S(2)}, u32[]{:S(2)}) collective-permute-start(f32[4,64,256]{2,1,0:T(8,128)S(1)} %own_far1.1), channel_id=1, source_target_pairs={{0,128},{64,192},{128,0},{192,64},{1,129},{65,193},{129,1},{193,65... | collective-permute-start | bytes 786440 | tf_op jit(solution)/shard_map/ppermute | solution.py:294
  29.3 13.2 %collective-permute-start.10 = (f32[4,64,256]{2,1,0:T(8,128)S(1)}, f32[4,64,256]{2,1,0:T(8,128)S(1)}, u32[]{:S(2)}, u32[]{:S(2)}) collective-permute-start(f32[4,64,256]{2,1,0:T(8,128)S(1)} %down1.1), channel_id=1, source_target_pairs={{1,0},{2,1},{3,2},{4,3},{5,4},{6,5},{7,6},{136,7},{9,8},{10,9},{11... | collective-permute-start | bytes 786440 | tf_op jit(solution)/shard_map/ppermute | solution.py:300
  37.6 6.5 %collective-permute-start.6 = (f32[4,64,256]{2,1,0:T(8,128)S(1)}, f32[4,64,256]{2,1,0:T(8,128)S(1)}, u32[]{:S(2)}, u32[]{:S(2)}) collective-permute-start(f32[4,64,256]{2,1,0:T(8,128)S(1)} %own_far0.1), channel_id=1, source_target_pairs={{0,128},{64,192},{128,0},{192,64},{1,129},{65,193},{129,1},{193,65... | collective-permute-start | bytes 786440 | tf_op jit(solution)/shard_map/ppermute | solution.py:294
